TPU v7x, 128 devices: a whole 4x4x4 slice. The times are simulated.
128 devices in a mesh: layer: 4 (over z_lo, core), lat: 32 (over z_hi, y, x).
Axes of the slice: x: 4, y: 4, z: 4 (z_hi: 2, z_lo: 2; z = z_hi * 2 + z_lo), core: 2. Of those that a mesh axis runs over, the one named last changes fastest.
Arguments:
- resid: bfloat16 [4, 256, 4608], P('layer', None, 'lat'), may hold values from -6 to 6
- target: bfloat16 [4, 256, 4608], P('layer', None, 'lat'), may hold values from -6 to 6
- enc_weight: bfloat16 [4, 4608, 8192], P('layer', None, 'lat'), may hold values from -0.09375 to 0.09375
- enc_bias: float32 [4, 8192], P('layer', 'lat'), may hold values from -3 to 3
- dec_weight: bfloat16 [4, 4, 8192, 4608], P('layer', None, 'lat'), may hold values from -0.125 to 0.125
- dec_bias: float32 [4, 4608], P('layer', 'lat'), may hold values from -3 to 3
Outputs:
- grad_enc: bfloat16 [4, 4608, 8192], P('layer', None, 'lat')
- grad_enc_bias: float32 [4, 8192], P('layer', 'lat')
- grad_dec: bfloat16 [4, 4, 8192, 4608], P('layer', None, 'lat')
- grad_dec_bias: float32 [4, 4608], P('layer', 'lat')
All inputs are finite; a program needn't handle non-finite values.
Results may differ from a plain program's by a relative error of at most 0.0085.
Values may be sent and summed in bfloat16 or wider, within the bound.
No kernel may reach another device: no remote copies, remote signals or barrier semaphores. Data moves between devices by JAX's collectives and lax.ppermute only.
A program may use at most 128 MiB of HBM per device.

v0:
```python
import jax
import jax.numpy as jnp
from jax import lax
from jax.sharding import PartitionSpec as P


def gelu_tanh(values):
    return jax.nn.gelu(values, approximate=True)


def body(resid, target, enc_weight, enc_bias, dec_weight, dec_bias):
    source = lax.axis_index("layer")
    tokens_all = resid.shape[1]
    n_targets = dec_weight.shape[1]
    factor = 2.0 / tokens_all
    rows_full = lax.all_gather(resid[0], "lat", axis=1, tiled=True)
    preact = jnp.dot(rows_full, enc_weight[0], preferred_element_type=jnp.float32) + enc_bias[0]
    latent = gelu_tanh(preact).astype(jnp.bfloat16)
    target_mask = (jnp.arange(n_targets, dtype=jnp.int32) >= source).astype(jnp.float32)
    partials = jnp.einsum("kf,tfd->ktd", latent, dec_weight[0], preferred_element_type=jnp.float32)
    partials = partials * target_mask[None, :, None]
    shared = lax.psum_scatter(partials, "lat", scatter_dimension=2, tiled=True)
    recon = lax.psum_scatter(shared, "layer", scatter_dimension=1, tiled=True)
    error = recon[:, 0, :] + dec_bias[0] - target[0].astype(jnp.float32)
    grad_dec_bias = (factor * jnp.sum(error, axis=0))[None]
    out_grad = (factor * error).astype(jnp.bfloat16)[:, None, :]
    features = lax.all_gather(out_grad, "lat", axis=2, tiled=True)
    all_grads = lax.all_gather(features, "layer", axis=1, tiled=True)
    masked_err = all_grads * target_mask.astype(jnp.bfloat16)[None, :, None]
    latent_grad = jnp.einsum(
        "ktd,tfd->kf", masked_err, dec_weight[0], preferred_element_type=jnp.float32
    )
    grad_dec = jnp.einsum(
        "kf,ktd->tfd", latent, masked_err, preferred_element_type=jnp.float32
    ).astype(jnp.bfloat16)[None]
    _, backward = jax.vjp(gelu_tanh, preact)
    pre_grad = backward(latent_grad)[0]
    grad_enc_bias = jnp.sum(pre_grad, axis=0)[None]
    grad_enc = lax.dot_general(
        rows_full,
        pre_grad.astype(jnp.bfloat16),
        (((0,), (0,)), ((), ())),
        preferred_element_type=jnp.float32,
    )
    grad_enc = grad_enc.astype(jnp.bfloat16)[None]
    return (grad_enc, grad_enc_bias, grad_dec, grad_dec_bias)


def solution(mesh):
    in_specs = (
        P("layer", None, "lat"),
        P("layer", None, "lat"),
        P("layer", None, "lat"),
        P("layer", "lat"),
        P("layer", None, "lat", None),
        P("layer", "lat"),
    )
    out_specs = (
        P("layer", None, "lat"),
        P("layer", "lat"),
        P("layer", None, "lat", None),
        P("layer", "lat"),
    )
    return jax.shard_map(body, mesh=mesh, in_specs=in_specs, out_specs=out_specs, check_vma=False)
```

profile of v0, /device:TPU:0, one launch (start us, length us, event | category | flops | bytes accessed | tf_op | source)
XLA Modules:
  0.0 610.8 jit_solution(15394293398689804027)
XLA Ops:
  7.2 0.0 copy-start
  7.2 0.0 all-gather.9.cloned.1.call-start
  7.2 0.7 all-gather.9.cloned.1.call-update
  7.9 0.0 reduce-scatter.3.cloned.1.call-start
  8.0 78.9 %all-gather.9.cloned.1.call-done = bf16[1,256,4608]{1,2,0:T(8,128)(2,1)} async-done(((bf16[1,256,144]{1,2,0:T(8,128)(2,1)}), bf16[1,256,4608]{1,2,0:T(8,128)(2,1)}) %all-gather.9.cloned.1.call-update) | async-done | bytes 2359312 | tf_op jit(solution)/shard_map/all_gather | solution.py:16
  86.9 0.0 copy-done
  86.9 2.5 fusion.20
  89.3 14.6 %convolution_multiply_fusion = f32[256,4,4608]{0,2,1:T(8,128)} fusion(bf16[1,4,256,4608]{3,2,1,0:T(8,128)(2,1)} %param.10, f32[4]{0:T(128)S(1)} %compare_convert_fusion, f32[256,256]{1,0:T(8,128)S(1)} %fusion.20), kind=kOutput, calls=%fused_computation | convolution fusion | flops 2421227520 | bytes 28573712 | tf_op jit(solution)/shard_map/kf,tfd->ktd/dot_general | solution.py:20
  104.0 0.0 copy-start.3
  104.0 0.0 copy-start.4
  104.0 0.0 reduce-scatter.3.cloned.1.call-update
  104.0 0.0 reduce-scatter.5.cloned.1.call-start
  104.1 275.8 %reduce-scatter.3.cloned.1.call-done = f32[256,4,144]{0,2,1:T(8,128)} async-done(((f32[256,4,4608]{0,2,1:T(8,128)}), f32[256,4,144]{0,2,1:T(8,128)}) %reduce-scatter.3.cloned.1.call-update) | async-done | bytes 589840 | tf_op jit(solution)/shard_map/reduce_scatter | solution.py:22
  379.9 0.0 reduce-scatter.5.cloned.1.call-update
  379.9 0.0 all-gather.5.cloned.1.call-start
  380.0 17.4 %reduce-scatter.5.cloned.1.call-done = f32[256,1,144]{0,2,1:T(8,128)} async-done(((f32[256,4,144]{0,2,1:T(8,128)}), f32[256,1,144]{0,2,1:T(8,128)}) %reduce-scatter.5.cloned.1.call-update) | async-done | bytes 147472 | tf_op jit(solution)/shard_map/reduce_scatter | solution.py:23
  397.3 0.0 copy-done.3
  397.3 0.0 copy-done.4
  397.3 1.6 fusion.37
  399.0 0.0 all-gather.5.cloned.1.call-update
  399.0 0.2 all-gather.7.cloned.1.call-start
  399.2 76.0 %all-gather.5.cloned.1.call-done = bf16[256,1,4608]{0,2,1:T(8,128)(2,1)} async-done(((bf16[256,1,144]{0,2,1:T(8,128)(2,1)}), bf16[256,1,4608]{0,2,1:T(8,128)(2,1)}) %all-gather.5.cloned.1.call-update) | async-done | bytes 2359312 | tf_op jit(solution)/shard_map/all_gather | solution.py:27
  475.2 4.3 copy.15
  479.5 0.0 all-gather.7.cloned.1.call-update
  479.5 1.1 fusion.39
  480.6 0.6 broadcast_multiply_fusion
  481.2 84.0 %all-gather.7.cloned.1.call-done = bf16[256,4,4608]{2,0,1:T(8,128)(2,1)} async-done(((bf16[256,1,4608]{2,0,1:T(8,128)(2,1)}), bf16[256,4,4608]{2,0,1:T(8,128)(2,1)}) %all-gather.7.cloned.1.call-update) | async-done | bytes 9437200 | tf_op jit(solution)/shard_map/all_gather | solution.py:28
  565.2 10.2 %fusion.5 = bf16[1,4,256,4608]{2,3,1,0:T(8,128)(2,1)} fusion(bf16[256,4,4608]{2,0,1:T(8,128)(2,1)} %all-gather.7.cloned.1.call-done, bf16[4]{0:T(256)(128)(2,1)S(1)} %fusion.43, f32[256,256]{1,0:T(8,128)S(1)} %fusion.20), kind=kOutput, calls=%fused_computation.7 | convolution fusion | flops 2425946112 | bytes 19136520 | tf_op jit(solution)/shard_map/kf,ktd->tfd/dot_general | solution.py:33
  575.4 12.6 %copy.18 = bf16[1,4,256,4608]{3,2,1,0:T(8,128)(2,1)} copy(bf16[1,4,256,4608]{2,3,1,0:T(8,128)(2,1)} %fusion.5) | data formatting | bytes 18874368
  588.0 0.0 copy-start.2
  588.0 0.0 copy-start.1
  588.0 9.8 %fusion.44 = (f32[256]{0:T(256)}, bf16[256,256]{1,0:T(8,128)(2,1)S(1)}) fusion(f32[256,256]{1,0:T(8,128)S(1)} %fusion.20, bf16[1,4,256,4608]{3,2,1,0:T(8,128)(2,1)} %param.10, bf16[256,4,4608]{2,0,1:T(8,128)(2,1)} %all-gather.7.cloned.1.call-done, bf16[4]{0:T(256)(128)(2,1)S(1)} %fusion.43), kind=kOutput, calls=%fused_computation.41 | convolution fusion | flops 2422013696 | bytes 19268616 | tf_op jit(solution)/shard_map/ktd,tfd->kf/dot_general | solution.py:30
  597.8 0.0 copy-done.2
  597.8 2.2 fusion.8
  600.0 4.3 copy.17
  604.3 0.0 copy-done.1
  (2 shorter events, 0.0 us)
Async XLA Ops:
  7.2 79.7 %copy-start = (bf16[1,4608,256]{2,1,0:T(8,128)(2,1)S(1)}, bf16[1,4608,256]{2,1,0:T(8,128)(2,1)}, u32[]{:S(2)}) copy-start(bf16[1,4608,256]{2,1,0:T(8,128)(2,1)} %param.8) | copy-start | bytes 7077892
  7.2 79.7 %all-gather.9.cloned.1.call-start = ((), (), s32[]{:S(2)}) async-start(), calls=%async_computation.6 | async-start | bytes 2433024 | tf_op jit(solution)/shard_map/all_gather | solution.py:16
  7.9 372.0 %reduce-scatter.3.cloned.1.call-start = ((), (), s32[]{:S(2)}) async-start(), calls=%async_computation.2 | async-start | bytes 19464192 | tf_op jit(solution)/shard_map/reduce_scatter | solution.py:22
  104.0 293.4 %copy-start.3 = (bf16[1,256,144]{1,2,0:T(8,128)(2,1)S(1)}, bf16[1,256,144]{1,2,0:T(8,128)(2,1)}, u32[]{:S(2)}) copy-start(bf16[1,256,144]{1,2,0:T(8,128)(2,1)} %param.7) | copy-start | bytes 221188
  104.0 293.4 %copy-start.4 = (f32[1,144]{1,0:T(1,128)S(1)}, f32[1,144]{1,0:T(1,128)}, u32[]{:S(2)}) copy-start(f32[1,144]{1,0:T(1,128)} %param.11) | copy-start | bytes 1732
  104.0 293.3 %reduce-scatter.5.cloned.1.call-start = ((), (), s32[]{:S(2)}) async-start(), calls=%async_computation.3 | async-start | bytes 737280 | tf_op jit(solution)/shard_map/reduce_scatter | solution.py:23
  379.9 95.3 %all-gather.5.cloned.1.call-start = ((), (), s32[]{:S(2)}) async-start(), calls=%async_computation.4 | async-start | bytes 2433024 | tf_op jit(solution)/shard_map/all_gather | solution.py:27
  399.0 166.2 %all-gather.7.cloned.1.call-start = ((), (), s32[]{:S(2)}) async-start(), calls=%async_computation.5 | async-start | bytes 11796480 | tf_op jit(solution)/shard_map/all_gather | solution.py:28
  588.0 9.8 %copy-start.2 = (bf16[1,256,4608]{1,2,0:T(8,128)(2,1)S(1)}, bf16[1,256,4608]{1,2,0:T(8,128)(2,1)}, u32[]{:S(2)}) copy-start(bf16[1,256,4608]{1,2,0:T(8,128)(2,1)} %all-gather.9.cloned.1.call-done) | copy-start | bytes 7077892
  588.0 16.3 %copy-start.1 = (bf16[1,4608,256]{2,1,0:T(8,128)(2,1)S(1)}, bf16[1,4608,256]{2,1,0:T(8,128)(2,1)}, u32[]{:S(2)}) copy-start(bf16[1,4608,256]{2,1,0:T(8,128)(2,1)} %param.8) | copy-start | bytes 7077892
Sparse Core Ops, SparseCore 0:
  11.0 75.8 all-gather.8
  104.1 275.7 reduce-scatter.2
  382.3 14.9 reduce-scatter.4
  400.7 74.4 all-gather.4
  479.6 85.5 all-gather.6
where the time goes:
time: 614 us; the launch traced here: 611 us
  waiting for transfers between devices  533 us (87%)
  matrix products  39.3 us (6%)
  local copies, waits for them, and re-layouts  21.2 us (3%)
  between operations  13.8 us (2%)
    reduce_scatter x1, waiting for transfers between devices, body(): shared = lax.psum_scatter(partials, 'lat', scatter_dimension=2, tiled=True)  276 us
    all_gather x1, waiting for transfers between devices, body(): all_grads = lax.all_gather(features, 'layer', axis=1, tiled=True)  84 us
    all_gather x1, waiting for transfers between devices, body(): rows_full = lax.all_gather(resid[0], 'lat', axis=1, tiled=True)  78.9 us
    all_gather x1, waiting for transfers between devices, body(): features = lax.all_gather(out_grad, 'lat', axis=2, tiled=True)  76 us
    reduce_scatter x1, waiting for transfers between devices, body(): recon = lax.psum_scatter(shared, 'layer', scatter_dimension=1, tiled=True)  17.4 us
    unnamed x12, local copies, waits for them, and re-layouts  16.9 us
    dot_general x1, matrix products, body(): jnp.einsum('kf,tfd->ktd', latent, dec_weight[0], preferred_element_type=j...  14.6 us
  transfers between devices with their start and end apart: 5, of which 5 were waited for; matrix products, arithmetic and copies ran while one was open for 0% of the time, Pallas kernels for 0%

commit v1 on v0

v1 whole, which is shorter than its diff:
```python
import jax
import jax.numpy as jnp
from jax import lax
from jax.sharding import Mesh, PartitionSpec as P

LAYER = ("zlo", "core")
LAT = ("zhi", "y", "x")
SAME_CORE = ("zlo", "zhi", "y", "x")


def gelu_tanh(values):
    return jax.nn.gelu(values, approximate=True)


def dot(a, b, ca, cb):
    return lax.dot_general(a, b, (((ca,), (cb,)), ((), ())), preferred_element_type=jnp.float32)


def gather_rows(block, axes, count):
    copies = jnp.broadcast_to(block[None], (count,) + block.shape)
    return lax.all_to_all(copies, axes, 0, 0, tiled=True)


def body(resid, target, enc_weight, enc_bias, dec_weight, dec_bias):
    zlo, core = lax.axis_index("zlo"), lax.axis_index("core")
    tokens = resid.shape[1]
    own_rows = resid.shape[2]
    lats = lax.axis_size("zhi") * lax.axis_size("y") * lax.axis_size("x")
    width = own_rows * lats
    factor = 2.0 / tokens
    dec = dec_weight[0]

    resid_t = gather_rows(resid[0].T, LAT, lats).reshape(width, tokens)
    preact = dot(enc_weight[0], resid_t, 0, 0) + enc_bias[0][:, None]
    latent = gelu_tanh(preact).astype(jnp.bfloat16)

    def partial(t):
        return dot(lax.dynamic_index_in_dim(dec, t, 0, keepdims=False), latent, 0, 0)

    give_late = partial(3 - core).astype(jnp.bfloat16)
    got_late = lax.ppermute(give_late, LAYER, [(0, 1), (1, 0), (2, 3)])
    give_early = partial(1 - core).astype(jnp.bfloat16)
    got_early = lax.ppermute(give_early, LAYER, [(0, 1)])
    early = partial(core) + got_early.astype(jnp.float32)
    early = jnp.where(zlo == 0, early, 0.0).astype(jnp.bfloat16)
    late = (partial(2 + core) + got_late.astype(jnp.float32)).astype(jnp.bfloat16)
    sums = jnp.stack([early, late]).reshape(2 * lats, own_rows, tokens)
    parts = lax.all_to_all(sums, SAME_CORE, 0, 0, tiled=True)
    recon = jnp.sum(parts.astype(jnp.float32), axis=0)

    error = recon + dec_bias[0][:, None] - target[0].T.astype(jnp.float32)
    grad_dec_bias = (factor * jnp.sum(error, axis=1))[None]
    out_grad = (factor * error).astype(jnp.bfloat16)

    grads = gather_rows(out_grad, SAME_CORE, 2 * lats).reshape(2, width, tokens)
    got_late_grad = lax.ppermute(grads[1], LAYER, [(0, 1), (1, 0), (3, 2)])
    got_early_grad = lax.ppermute(grads[0], LAYER, [(1, 0)])
    layer = 2 * zlo + core
    first, second = jnp.where(core == 0, grads[0], got_early_grad), jnp.where(core == 0, got_early_grad, grads[0])
    third, fourth = jnp.where(core == 0, grads[1], got_late_grad), jnp.where(core == 0, got_late_grad, grads[1])
    latent_grad = 0.0
    grad_dec = []
    for t, grad in enumerate((first, second, third, fourth)):
        grad = jnp.where(t >= layer, grad, jnp.zeros_like(grad))
        latent_grad = latent_grad + dot(dec[t], grad, 1, 0)
        grad_dec.append(dot(latent, grad, 1, 1).astype(jnp.bfloat16))
    grad_dec = jnp.stack(grad_dec)[None]

    _, backward = jax.vjp(gelu_tanh, preact)
    pre_grad = backward(latent_grad)[0]
    grad_enc_bias = jnp.sum(pre_grad, axis=1)[None]
    grad_enc = dot(resid_t, pre_grad.astype(jnp.bfloat16), 1, 1).astype(jnp.bfloat16)[None]
    return (grad_enc, grad_enc_bias, grad_dec, grad_dec_bias)


def solution(mesh):
    fine = Mesh(mesh.devices.reshape(2, 2, 2, 4, 4), LAYER + LAT)
    in_specs = (
        P(LAYER, None, LAT),
        P(LAYER, None, LAT),
        P(LAYER, None, LAT),
        P(LAYER, LAT),
        P(LAYER, None, LAT, None),
        P(LAYER, LAT),
    )
    out_specs = (
        P(LAYER, None, LAT),
        P(LAYER, LAT),
        P(LAYER, None, LAT, None),
        P(LAYER, LAT),
    )
    return jax.shard_map(body, mesh=fine, in_specs=in_specs, out_specs=out_specs, check_vma=False)
```

time: 614 us -> 239 us (0.39)
  waiting for transfers between devices: 533 us -> 35.1 us
  blocking collectives: 0 us -> 128 us
  starting transfers between devices: 0.38 us -> 20.1 us
  local copies, waits for them, and re-layouts: 21.2 us -> 7.3 us
  between operations: 13.8 us -> 0.9 us
    reduce_scatter x2 -> x0, waiting for transfers between devices: 293 us -> none  [the longest x1 276 us: body(): shared = lax.psum_scatter(partials, 'lat', scatter_dimension=2, tiled=True)]
    all_gather x3 -> x0, waiting for transfers between devices: 239 us -> none  [the longest x1 84 us: body(): all_grads = lax.all_gather(features, 'layer', axis=1, tiled=True)]
    all_to_all x0 -> x2, blocking collectives: none -> 128 us  [the longest x1 65.1 us: body(): parts = lax.all_to_all(sums, SAME_CORE, 0, 0, tiled=True)]
    all_to_all x0 -> x1, waiting for transfers between devices: none -> 32.3 us  [gather_rows(): return lax.all_to_all(copies, axes, 0, 0, tiled=True)]
    unnamed x12 -> x21, local copies, waits for them, and re-layouts: 16.9 us -> 2.69 us
    all_to_all x0 -> x1, starting transfers between devices: none -> 11 us  [gather_rows(): return lax.all_to_all(copies, axes, 0, 0, tiled=True)]
    ppermute x0 -> x4, starting transfers between devices: none -> 9.15 us  [the longest x1 3.84 us: body(): got_early = lax.ppermute(give_early, LAYER, [(0, 1)])]
    dot_general x5 -> x14, matrix products: 39.3 us -> 39.2 us  [dot(): lax.dot_general(a, b, (((ca,), (cb,)), ((), ())), preferred_element_type=...]
  transfers between devices with their start and end apart: 5 -> 5, of which waited for: 5 -> 2; matrix products, arithmetic and copies ran while one was open for 0% -> 6% of each run, Pallas kernels for 0% -> 0%
where the time goes in v1:
time: 239 us; the launch traced here: 237 us
  blocking collectives  128 us (54%)
  matrix products  39.2 us (16%)
  waiting for transfers between devices  35.1 us (15%)
  starting transfers between devices  20.1 us (8%)
  local copies, waits for them, and re-layouts  7.3 us (3%)
  other arithmetic  6.06 us (3%)
    all_to_all x1, blocking collectives, body(): parts = lax.all_to_all(sums, SAME_CORE, 0, 0, tiled=True)  65.1 us
    all_to_all x1, blocking collectives, gather_rows(): return lax.all_to_all(copies, axes, 0, 0, tiled=True)  63.3 us
    dot_general x14, matrix products, dot(): lax.dot_general(a, b, (((ca,), (cb,)), ((), ())), preferred_element_type=...  39.2 us
    all_to_all x1, waiting for transfers between devices, gather_rows(): return lax.all_to_all(copies, axes, 0, 0, tiled=True)  32.3 us
    all_to_all x1, starting transfers between devices, gather_rows(): return lax.all_to_all(copies, axes, 0, 0, tiled=True)  11 us
  transfers between devices with their start and end apart: 5, of which 2 were waited for; matrix products, arithmetic and copies ran while one was open for 6% of the time, Pallas kernels for 0%

profile of v1, /device:TPU:0, one launch (start us, length us, event | category | flops | bytes accessed | tf_op | source)
XLA Modules:
  0.0 237.1 jit_solution(10344971612726528830)
XLA Ops:
  0.6 0.0 copy-start
  0.6 2.6 %broadcast_in_dim.26 = bf16[32,144,256]{2,1,0:T(8,128)(2,1)} broadcast(bf16[144,256]{1,0:T(8,128)(2,1)} %bitcast.111), dimensions={1,2} | broadcast | bytes 2433024 | tf_op jit(solution)/shard_map/broadcast_in_dim | solution.py:20
  3.2 11.0 %all-to-all-start = ((bf16[32,144,256]{2,1,0:T(8,128)(2,1)}), bf16[32,144,256]{2,1,0:T(8,128)(2,1)}, u32[]{:S(2)}, u32[]{:S(2)}) async-start(bf16[32,144,256]{2,1,0:T(8,128)(2,1)} %broadcast_in_dim.26), calls=%async_computation | async-start | bytes 4718592 | tf_op jit(solution)/shard_map/all_to_all | solution.py:21
  14.2 32.3 %all-to-all-done = bf16[32,144,256]{2,1,0:T(8,128)(2,1)} async-done(((bf16[32,144,256]{2,1,0:T(8,128)(2,1)}), bf16[32,144,256]{2,1,0:T(8,128)(2,1)}, u32[]{:S(2)}, u32[]{:S(2)}) %all-to-all-start) | async-done | bytes 2359328 | tf_op jit(solution)/shard_map/all_to_all | solution.py:21
  46.5 0.0 copy-done
  46.5 0.0 copy-done.6
  46.5 2.7 %multiply_convert_fusion = (bf16[256,256]{0,1:T(8,128)(2,1)S(1)}, f32[256,256]{0,1:T(8,128)S(1)}) fusion(f32[256]{0:T(256)S(1)} %bitcast.114, bf16[4608,256]{1,0:T(8,128)(2,1)} %bitcast.4, bf16[1,4608,256]{2,1,0:T(8,128)(2,1)S(1)} %copy-done), kind=kOutput, calls=%fused_computation.60 | convolution fusion | flops 604635136 | bytes 5112832 | tf_op jit(solution)/shard_map/dot_general | solution.py:16
  49.3 2.5 %convolution_convert_fusion.5 = bf16[4608,256]{1,0:T(8,128)(2,1)S(1)} fusion(bf16[256,256]{0,1:T(8,128)(2,1)S(1)} %get-tuple-element.12, bf16[1,4,256,4608]{3,2,1,0:T(8,128)(2,1)} %param.10, s32[]{:T(128)S(6)} %select_n.72), kind=kOutput, calls=%fused_computation.7 | convolution fusion | flops 605159424 | bytes 4849668 | tf_op jit(solution)/shard_map/dot_general | solution.py:16
  51.8 1.9 collective-permute-start.1
  53.7 3.9 %convolution_convert_fusion.6 = bf16[4608,256]{1,0:T(8,128)(2,1)} fusion(bf16[256,256]{0,1:T(8,128)(2,1)S(1)} %get-tuple-element.12, bf16[1,4,256,4608]{3,2,1,0:T(8,128)(2,1)} %param.10, s32[]{:T(128)S(6)} %select_n.69), kind=kOutput, calls=%fused_computation.8 | convolution fusion | flops 605159424 | bytes 4849668 | tf_op jit(solution)/shard_map/dot_general | solution.py:16
  57.6 3.8 %collective-permute-start = (bf16[4608,256]{1,0:T(8,128)(2,1)}, bf16[4608,256]{1,0:T(8,128)(2,1)}, u32[]{:S(2)}, u32[]{:S(2)}) collective-permute-start(bf16[4608,256]{1,0:T(8,128)(2,1)} %convolution_convert_fusion.6), channel_id=1, source_target_pairs={{0,32},{1,33},{2,34},{3,35},{4,36},{5,37},{6,38},{7,39},{8,40},{9,... | collective-permute-start | bytes 7077896 | tf_op jit(solution)/shard_map/ppermute | solution.py:43
  61.5 0.0 collective-permute-done.1
  61.5 3.2 %fusion.6 = bf16[1,4608,256]{2,1,0:T(8,128)(2,1)S(1)} fusion(bf16[4608,256]{1,0:T(8,128)(2,1)} %collective-permute-done.1, bf16[256,256]{0,1:T(8,128)(2,1)S(1)} %get-tuple-element.12, bf16[1,4,256,4608]{3,2,1,0:T(8,128)(2,1)} %param.10, s32[]{:T(128)S(6)} %select_n.71), kind=kOutput, calls=%fused_computation.18 | convolution fusion | flops 607518720 | bytes 7208964 | tf_op jit(solution)/shard_map/dot_general | solution.py:16
  64.7 0.0 collective-permute-done
  64.7 3.2 %fusion.5 = bf16[1,4608,256]{2,1,0:T(8,128)(2,1)S(1)} fusion(bf16[4608,256]{1,0:T(8,128)(2,1)} %collective-permute-done, bf16[256,256]{0,1:T(8,128)(2,1)S(1)} %get-tuple-element.12, bf16[1,4,256,4608]{3,2,1,0:T(8,128)(2,1)} %param.10, s32[]{:T(128)S(6)} %select_n.68, pred[]{:T(512)S(6)} %eq.10), kind=kOutput, calls=%fused_computation.17 | convolution fusion | flops 608698368 | bytes 7208965 | tf_op jit(solution)/shard_map/dot_general | solution.py:16
  67.9 0.4 pad_maximum_fusion
  68.4 65.1 %all_to_all.15 = bf16[64,144,256]{2,1,0:T(8,128)(2,1)S(1)} all-to-all(bf16[64,144,256]{2,1,0:T(8,128)(2,1)S(1)} %bitcast.103), channel_id=1, replica_groups=mesh['zlo'=2,'core'=2,'zhi'=2,'y'=4,'x'=4] {'zlo','zhi','y','x'}, dimensions={0} | all-to-all | bytes 9437184 | tf_op jit(solution)/shard_map/all_to_all | solution.py:48
  133.5 0.7 convert_reduce_fusion
  134.2 0.2 copy-done.4
  134.4 0.0 copy-done.5
  134.4 0.2 fusion.60
  134.6 0.3 broadcast_in_dim.28
  134.9 63.3 %all_to_all.16 = bf16[64,144,256]{2,1,0:T(8,128)(2,1)S(1)} all-to-all(bf16[64,144,256]{2,1,0:T(8,128)(2,1)S(1)} %broadcast_in_dim.28), channel_id=1, replica_groups=mesh['zlo'=2,'core'=2,'zhi'=2,'y'=4,'x'=4] {'zlo','zhi','y','x'}, dimensions={0} | all-to-all | bytes 9437184 | tf_op jit(solution)/shard_map/all_to_all | solution.py:21
  198.2 1.7 fusion.73
  199.9 1.9 collective-permute-start.3
  201.8 1.5 collective-permute-start.2
  203.3 0.6 broadcast_multiply_fusion
  203.9 2.8 %collective-permute-done.3 = bf16[4608,256]{1,0:T(8,128)(2,1)} collective-permute-done((bf16[4608,256]{1,0:T(8,128)(2,1)}, bf16[4608,256]{1,0:T(8,128)(2,1)}, u32[]{:S(2)}, u32[]{:S(2)}) %collective-permute-start.3) | collective-permute-done | bytes 2359328 | tf_op jit(solution)/shard_map/ppermute | solution.py:56
  206.6 3.8 %fusion.7 = f32[256,256]{1,0:T(8,128)S(1)} fusion(bf16[1,4,256,4608]{3,2,1,0:T(8,128)(2,1)} %param.10, bf16[4608,256]{1,0:T(8,128)(2,1)} %collective-permute-done.3, bf16[4608,256]{1,0:T(8,128)(2,1)} %bitcast.18, pred[]{:T(512)S(6)} %le.15, pred[]{:T(512)S(6)} %eq.4), kind=kOutput, calls=%fused_computation.19 | convolution fusion | flops 606339072 | bytes 7340034 | tf_op jit(solution)/shard_map/dot_general | solution.py:16
  210.4 0.0 slice-start.2
  210.5 3.8 %fusion.9 = f32[256,256]{1,0:T(8,128)S(1)} fusion(bf16[1,4,256,4608]{3,2,1,0:T(8,128)(2,1)} %param.10, bf16[4608,256]{1,0:T(8,128)(2,1)} %bitcast.18, bf16[4608,256]{1,0:T(8,128)(2,1)} %collective-permute-done.3, pred[]{:T(512)S(6)} %le.14, pred[]{:T(512)S(6)} %eq.4), kind=kOutput, calls=%fused_computation.21 | convolution fusion | flops 606339072 | bytes 7340034 | tf_op jit(solution)/shard_map/dot_general | solution.py:16
  214.2 0.0 collective-permute-done.2
  214.2 0.0 slice-done
  214.2 0.0 slice-done.1
  214.2 0.0 slice-done.2
  214.3 3.0 %fusion.11 = f32[256,256]{1,0:T(8,128)S(1)} fusion(bf16[1,4,256,4608]{3,2,1,0:T(8,128)(2,1)S(1)} %bitcast.105, bf16[4608,256]{1,0:T(8,128)(2,1)} %collective-permute-done.2, bf16[4608,256]{1,0:T(8,128)(2,1)S(1)} %bitcast.107, pred[]{:T(512)S(6)} %le.13, pred[]{:T(512)S(6)} %eq.4), kind=kOutput, calls=%fused_computation.23 | convolution fusion | flops 606339072 | bytes 7340034 | tf_op jit(solution)/shard_map/dot_general | solution.py:16
  217.3 0.0 copy-done.2
  217.3 2.1 fusion.74
  219.3 2.5 %fusion = bf16[1,4608,256]{1,2,0:T(8,128)(2,1)S(1)} fusion(bf16[4608,256]{1,0:T(8,128)(2,1)} %bitcast.4, bf16[256,256]{0,1:T(8,128)(2,1)S(1)} %get-tuple-element.15), kind=kOutput, calls=%fused_computation.9 | convolution fusion | flops 605159424 | bytes 4849664 | tf_op jit(solution)/shard_map/dot_general | solution.py:16
  221.8 2.4 %copy.10 = bf16[1,4608,256]{2,1,0:T(8,128)(2,1)} copy(bf16[1,4608,256]{1,2,0:T(8,128)(2,1)S(1)} %fusion) | data formatting | bytes 4718592
  224.3 2.5 %fusion.3 = bf16[1,256,4608]{2,1,0:T(8,128)(2,1)S(1)} fusion(bf16[256,256]{0,1:T(8,128)(2,1)S(1)} %get-tuple-element.12, bf16[4608,256]{1,0:T(8,128)(2,1)} %bitcast.18, bf16[4608,256]{1,0:T(8,128)(2,1)} %collective-permute-done.3, pred[]{:T(512)S(6)} %le.14, pred[]{:T(512)S(6)} %eq.4), kind=kOutput, calls=%fused_computation.12 | convolution fusion | flops 607518720 | bytes 7208962 | tf_op jit(solution)/shard_map/dot_general | solution.py:16
  226.8 0.0 copy-start.3
  226.8 2.7 %fusion.4 = bf16[1,256,4608]{2,1,0:T(8,128)(2,1)S(1)} fusion(bf16[256,256]{0,1:T(8,128)(2,1)S(1)} %get-tuple-element.12, bf16[4608,256]{1,0:T(8,128)(2,1)} %collective-permute-done.3, bf16[4608,256]{1,0:T(8,128)(2,1)} %bitcast.18, pred[]{:T(512)S(6)} %le.15, pred[]{:T(512)S(6)} %eq.4), kind=kOutput, calls=%fused_computation.13 | convolution fusion | flops 607518720 | bytes 7208962 | tf_op jit(solution)/shard_map/dot_general | solution.py:16
  229.5 0.0 copy-done.3
  229.5 0.8 fusion.1
  230.3 2.5 %fusion.2 = bf16[1,256,4608]{2,1,0:T(8,128)(2,1)S(1)} fusion(bf16[256,256]{0,1:T(8,128)(2,1)S(1)} %get-tuple-element.12, bf16[4608,256]{1,0:T(8,128)(2,1)} %collective-permute-done.2, bf16[4608,256]{1,0:T(8,128)(2,1)S(1)} %bitcast.110, pred[]{:T(512)S(6)} %le.13, pred[]{:T(512)S(6)} %eq.4), kind=kOutput, calls=%fused_computation.11 | convolution fusion | flops 607518720 | bytes 7208962 | tf_op jit(solution)/shard_map/dot_general | solution.py:16
  232.8 0.0 copy-start.1
  232.9 4.2 %maximum_bitcast_fusion = bf16[1,4,256,4608]{3,2,1,0:T(8,128)(2,1)} fusion(bf16[1,256,4608]{2,1,0:T(8,128)(2,1)S(1)} %fusion.4, bf16[1,256,4608]{2,1,0:T(8,128)(2,1)S(1)} %fusion.3, bf16[1,256,4608]{2,1,0:T(8,128)(2,1)S(1)} %fusion.2, bf16[1,256,4608]{2,1,0:T(8,128)(2,1)S(1)} %fusion.1), kind=kLoop, calls=%fused_computation | loop fusion | flops 14155776 | bytes 18874368 | tf_op jit(solution)/shard_map/broadcast_in_dim | solution.py:67
  (8 shorter events, 0.0 us)
Async XLA Ops:
  0.6 45.9 %copy-start = (bf16[1,4608,256]{2,1,0:T(8,128)(2,1)S(1)}, bf16[1,4608,256]{2,1,0:T(8,128)(2,1)}, u32[]{:S(2)}) copy-start(bf16[1,4608,256]{2,1,0:T(8,128)(2,1)} %param.8) | copy-start | bytes 7077892
  3.2 43.3 %copy-start.6 = (f32[1,256]{1,0:T(1,128)S(1)}, f32[1,256]{1,0:T(1,128)}, u32[]{:S(2)}) copy-start(f32[1,256]{1,0:T(1,128)} %param.9) | copy-start | bytes 3076
  3.2 43.3 %all-to-all-start = ((bf16[32,144,256]{2,1,0:T(8,128)(2,1)}), bf16[32,144,256]{2,1,0:T(8,128)(2,1)}, u32[]{:S(2)}, u32[]{:S(2)}) async-start(bf16[32,144,256]{2,1,0:T(8,128)(2,1)} %broadcast_in_dim.26), calls=%async_computation | async-start | bytes 4718592 | tf_op jit(solution)/shard_map/all_to_all | solution.py:21
  51.8 9.7 %collective-permute-start.1 = (bf16[4608,256]{1,0:T(8,128)(2,1)S(1)}, bf16[4608,256]{1,0:T(8,128)(2,1)}, u32[]{:S(2)}, u32[]{:S(2)}) collective-permute-start(bf16[4608,256]{1,0:T(8,128)(2,1)S(1)} %convolution_convert_fusion.5), channel_id=1, source_target_pairs={{0,32},{32,0},{64,96},{1,33},{33,1},{65,97},{2,34},{34,2},{66,98},... | collective-permute-start | bytes 7077896 | tf_op jit(solution)/shard_map/ppermute | solution.py:41
  57.6 7.1 %collective-permute-start = (bf16[4608,256]{1,0:T(8,128)(2,1)}, bf16[4608,256]{1,0:T(8,128)(2,1)}, u32[]{:S(2)}, u32[]{:S(2)}) collective-permute-start(bf16[4608,256]{1,0:T(8,128)(2,1)} %convolution_convert_fusion.6), channel_id=1, source_target_pairs={{0,32},{1,33},{2,34},{3,35},{4,36},{5,37},{6,38},{7,39},{8,40},{9,... | collective-permute-start | bytes 7077896 | tf_op jit(solution)/shard_map/ppermute | solution.py:43
  133.5 0.9 copy-start.4
  133.5 0.9 copy-start.5
  199.9 17.4 %copy-start.2 = (bf16[32,144,256]{2,1,0:T(8,128)(2,1)}, bf16[32,144,256]{2,1,0:T(8,128)(2,1)S(1)}, u32[]{:S(2)}) copy-start(bf16[32,144,256]{2,1,0:T(8,128)(2,1)S(1)} %get-tuple-element.8) | copy-start | bytes 7077892
  199.9 6.8 %collective-permute-start.3 = (bf16[4608,256]{1,0:T(8,128)(2,1)}, bf16[4608,256]{1,0:T(8,128)(2,1)}, u32[]{:S(2)}, u32[]{:S(2)}) collective-permute-start(bf16[4608,256]{1,0:T(8,128)(2,1)} %bitcast.18), channel_id=1, source_target_pairs={{0,32},{32,0},{96,64},{1,33},{33,1},{97,65},{2,34},{34,2},{98,66},... | collective-permute-start | bytes 7077896 | tf_op jit(solution)/shard_map/ppermute | solution.py:56
  201.8 12.4 %collective-permute-start.2 = (bf16[4608,256]{1,0:T(8,128)(2,1)S(1)}, bf16[4608,256]{1,0:T(8,128)(2,1)}, u32[]{:S(2)}, u32[]{:S(2)}) collective-permute-start(bf16[4608,256]{1,0:T(8,128)(2,1)S(1)} %bitcast.106), channel_id=1, source_target_pairs={{32,0},{33,1},{34,2},{35,3},{36,4},{37,5},{38,6},{39,7},{40,8},{41... | collective-permute-start | bytes 7077896 | tf_op jit(solution)/shard_map/ppermute | solution.py:57
  206.6 7.6 %slice-start = ((s8[9437184]{0:T(1024)(128)(4,1)}), s8[4194304]{0:T(1024)(128)(4,1)S(1)}, s32[]{:S(2)}) async-start(s8[9437184]{0:T(1024)(128)(4,1)} %bitcast.104), calls=%async_computation.3 | async-start | bytes 8388608
  206.6 7.6 %slice-start.1 = ((s8[9437184]{0:T(1024)(128)(4,1)}), s8[4194304]{0:T(1024)(128)(4,1)S(1)}, s32[]{:S(2)}) async-start(s8[9437184]{0:T(1024)(128)(4,1)} %bitcast.104), calls=%async_computation.4 | async-start | bytes 8388608
  210.4 3.8 %slice-start.2 = ((s8[9437184]{0:T(1024)(128)(4,1)}), s8[1048576]{0:T(1024)(128)(4,1)S(1)}, s32[]{:S(2)}) async-start(s8[9437184]{0:T(1024)(128)(4,1)} %bitcast.104), calls=%async_computation.5 | async-start | bytes 2097152
  226.8 2.7 %copy-start.3 = (bf16[32,144,256]{2,1,0:T(8,128)(2,1)S(1)}, bf16[32,144,256]{2,1,0:T(8,128)(2,1)}, u32[]{:S(2)}) copy-start(bf16[32,144,256]{2,1,0:T(8,128)(2,1)} %copy-done.2) | copy-start | bytes 7077892
  232.8 4.2 %copy-start.1 = (bf16[1,4608,256]{2,1,0:T(8,128)(2,1)S(1)}, bf16[1,4608,256]{2,1,0:T(8,128)(2,1)}, u32[]{:S(2)}) copy-start(bf16[1,4608,256]{2,1,0:T(8,128)(2,1)} %param.8) | copy-start | bytes 7077892

commit v2 on v1

--- a/solution.py
+++ b/solution.py
@@ -1,6 +1,10 @@
+import math
+
 import jax
 import jax.numpy as jnp
 from jax import lax
+from jax.experimental import pallas as pl
+from jax.experimental.pallas import tpu as pltpu
 from jax.sharding import Mesh, PartitionSpec as P
 
 LAYER = ("zlo", "core")
@@ -19,6 +23,126 @@
 def gather_rows(block, axes, count):
     copies = jnp.broadcast_to(block[None], (count,) + block.shape)
     return lax.all_to_all(copies, axes, 0, 0, tiled=True)
+
+
+def gelu_slope(x):
+    scale, cubic = math.sqrt(2.0 / math.pi), 0.044715
+    bent = jnp.tanh(scale * (x + cubic * x * x * x))
+    return 0.5 * (1.0 + bent) + 0.5 * x * (1.0 - bent * bent) * scale * (1.0 + 3.0 * cubic * x * x)
+
+
+def slot_step(plan, dec_ref, early_ref, late_ref, latent_ref, grad_dec_ref, total_ref):
+    slot = pl.program_id(0)
+    live = plan[2 * slot + 1] == 1
+
+    def work(grad_ref):
+        grad = grad_ref[...]
+        total_ref[...] += dot(dec_ref[0], grad, 1, 0)
+        grad_dec_ref[0] = dot(latent_ref[...], grad, 1, 1).astype(jnp.bfloat16)
+
+    pl.when(live & (slot == 0))(lambda: work(early_ref))
+    pl.when(live & (slot == 1))(lambda: work(late_ref))
+
+    @pl.when(jnp.logical_not(live))
+    def _():
+        grad_dec_ref[...] = jnp.zeros_like(grad_dec_ref)
+
+
+def own_kernel(plan, dec_ref, early_ref, late_ref, latent_ref, grad_dec_ref, total_ref):
+    @pl.when((pl.program_id(0) == 0) & (pl.program_id(1) == 0))
+    def _():
+        total_ref[...] = jnp.zeros_like(total_ref)
+
+    slot_step(plan, dec_ref, early_ref, late_ref, latent_ref, grad_dec_ref, total_ref)
+
+
+def other_kernel(plan, dec_ref, early_ref, late_ref, latent_ref, start_ref, preact_ref, _, grad_dec_ref, pre_ref,
+                 bias_ref, total_ref):
+    slot, tile = pl.program_id(0), pl.program_id(1)
+
+    @pl.when((slot == 0) & (tile == 0))
+    def _():
+        total_ref[...] = start_ref[...]
+
+    slot_step(plan, dec_ref, early_ref, late_ref, latent_ref, grad_dec_ref, total_ref)
+
+    @pl.when((slot == 1) & (tile == pl.num_programs(1) - 1))
+    def _():
+        pre_grad = total_ref[...] * gelu_slope(preact_ref[...])
+        bias_ref[...] = jnp.sum(pre_grad, axis=1, keepdims=True)
+        pre_ref[...] = pre_grad.astype(jnp.bfloat16)
+
+
+TILE = 1152
+PARAMS = dict(dimension_semantics=("arbitrary", "arbitrary"), vmem_limit_bytes=32 * 1024 * 1024)
+
+
+def slot_specs(rows, tokens, width):
+    tiles = width // TILE
+
+    def dec_map(slot, tile, plan):
+        return plan[2 * slot], 0, tile * plan[2 * slot + 1]
+
+    dec_spec = pl.BlockSpec((1, rows, TILE), dec_map)
+    early_spec = pl.BlockSpec(
+        (TILE, tokens), lambda slot, tile, plan: (jnp.where(slot == 0, tile, tiles - 1) * plan[1], 0))
+    late_spec = pl.BlockSpec((TILE, tokens), lambda slot, tile, plan: (jnp.where(slot == 0, 0, tile) * plan[3], 0))
+    out_spec = pl.BlockSpec((1, rows, TILE), lambda slot, tile, plan: (plan[2 * slot], 0, tile))
+    return tiles, dec_spec, early_spec, late_spec, out_spec
+
+
+def whole(*shape):
+    return pl.BlockSpec(shape, lambda slot, tile, plan: (0,) * len(shape))
+
+
+def cost(dec):
+    _, rows, width = dec.shape
+    return pl.CostEstimate(flops=8 * rows * width * 256, bytes_accessed=6 * rows * width * 2, transcendentals=0)
+
+
+def backward_own(plan, dec, early, late, latent):
+    _, rows, width = dec.shape
+    tokens = latent.shape[1]
+    tiles, dec_spec, early_spec, late_spec, out_spec = slot_specs(rows, tokens, width)
+    return pl.pallas_call(
+        own_kernel,
+        grid_spec=pltpu.PrefetchScalarGridSpec(
+            num_scalar_prefetch=1,
+            grid=(2, tiles),
+            in_specs=[dec_spec, early_spec, late_spec, whole(rows, tokens)],
+            out_specs=[out_spec, whole(rows, tokens)],
+        ),
+        out_shape=[jax.ShapeDtypeStruct(dec.shape, jnp.bfloat16), jax.ShapeDtypeStruct((rows, tokens), jnp.float32)],
+        compiler_params=pltpu.CompilerParams(**PARAMS),
+        cost_estimate=cost(dec),
+        name="backward_own",
+    )(plan, dec, early, late, latent)
+
+
+def backward_other(plan, dec, early, late, latent, start, preact, grad_dec):
+    _, rows, width = dec.shape
+    tokens = latent.shape[1]
+    tiles, dec_spec, early_spec, late_spec, out_spec = slot_specs(rows, tokens, width)
+    return pl.pallas_call(
+        other_kernel,
+        grid_spec=pltpu.PrefetchScalarGridSpec(
+            num_scalar_prefetch=1,
+            grid=(2, tiles),
+            in_specs=[dec_spec, early_spec, late_spec, whole(rows, tokens), whole(rows, tokens), whole(rows, tokens),
+                      pl.BlockSpec(memory_space=pl.ANY)],
+            out_specs=[out_spec, whole(rows, tokens), whole(rows, 1)],
+            scratch_shapes=[pltpu.VMEM((rows, tokens), jnp.float32)],
+        ),
+        out_shape=[
+            jax.ShapeDtypeStruct(dec.shape, jnp.bfloat16),
+            jax.ShapeDtypeStruct((rows, tokens), jnp.bfloat16),
+            jax.ShapeDtypeStruct((rows, 1), jnp.float32),
+        ],
+        input_output_aliases={7: 0},
+        compiler_params=pltpu.CompilerParams(**PARAMS),
+        cost_estimate=cost(dec),
+        name="backward_other",
+    )(plan, dec, early, late, latent, start, preact, grad_dec)
 
 
 def body(resid, target, enc_weight, enc_bias, dec_weight, dec_bias):
@@ -55,22 +179,16 @@
     grads = gather_rows(out_grad, SAME_CORE, 2 * lats).reshape(2, width, tokens)
     got_late_grad = lax.ppermute(grads[1], LAYER, [(0, 1), (1, 0), (3, 2)])
     got_early_grad = lax.ppermute(grads[0], LAYER, [(1, 0)])
-    layer = 2 * zlo + core
-    first, second = jnp.where(core == 0, grads[0], got_early_grad), jnp.where(core == 0, got_early_grad, grads[0])
-    third, fourth = jnp.where(core == 0, grads[1], got_late_grad), jnp.where(core == 0, got_late_grad, grads[1])
-    latent_grad = 0.0
-    grad_dec = []
-    for t, grad in enumerate((first, second, third, fourth)):
-        grad = jnp.where(t >= layer, grad, jnp.zeros_like(grad))
-        latent_grad = latent_grad + dot(dec[t], grad, 1, 0)
-        grad_dec.append(dot(latent, grad, 1, 1).astype(jnp.bfloat16))
-    grad_dec = jnp.stack(grad_dec)[None]
-
-    _, backward = jax.vjp(gelu_tanh, preact)
-    pre_grad = backward(latent_grad)[0]
-    grad_enc_bias = jnp.sum(pre_grad, axis=1)[None]
-    grad_enc = dot(resid_t, pre_grad.astype(jnp.bfloat16), 1, 1).astype(jnp.bfloat16)[None]
-    return (grad_enc, grad_enc_bias, grad_dec, grad_dec_bias)
+
+    on = jnp.int32(1)
+    own_plan = jnp.stack([core, (zlo == 0).astype(jnp.int32), 2 + core, on])
+    other_plan = jnp.stack([1 - core, ((zlo == 0) & (core == 0)).astype(jnp.int32),
+                            3 - core, ((zlo == 0) | (core == 0)).astype(jnp.int32)])
+    grad_dec, latent_grad = backward_own(own_plan, dec, grads[0], grads[1], latent)
+    grad_dec, pre_grad, bias_grad = backward_other(
+        other_plan, dec, got_early_grad, got_late_grad, latent, latent_grad, preact, grad_dec)
+    grad_enc = dot(resid_t, pre_grad, 1, 1).astype(jnp.bfloat16)[None]
+    return (grad_enc, bias_grad.reshape(1, -1), grad_dec[None], grad_dec_bias)
 
 
 def solution(mesh):

time: 239 us -> 238 us (level)
  matrix products: 39.2 us -> 19.4 us
  Pallas kernels: 0 us -> 18.4 us
  local copies, waits for them, and re-layouts: 7.3 us -> 12.8 us
  other arithmetic: 6.06 us -> 2.7 us
  waiting for transfers between devices: 35.1 us -> 32.3 us
  starting transfers between devices: 20.1 us -> 22.6 us
    dot_general x14 -> x6, matrix products: 39.2 us -> 19.4 us  [dot(): lax.dot_general(a, b, (((ca,), (cb,)), ((), ())), preferred_element_type=...]
    pallas_call x0 -> x2, Pallas kernels: none -> 18.4 us  [the longest x1 9.69 us: backward_other(): pl.pallas_call(other_kernel, grid_spec=pltpu.PrefetchScalarGridSpec(num_s...]
    unnamed x21 -> x13, local copies, waits for them, and re-layouts: 2.69 us -> 8.18 us
    broadcast_in_dim x1 -> x0, other arithmetic: 4.2 us -> none  [body(): grad_dec = jnp.stack(grad_dec)[None]]
    ppermute x1, waiting for transfers between devices: 2.78 us -> 0.01 us  [body(): got_late_grad = lax.ppermute(grads[1], LAYER, [(0, 1), (1, 0), (3, 2)])]
    ppermute x1, starting transfers between devices: 1.91 us -> 4.62 us  [body(): got_late_grad = lax.ppermute(grads[1], LAYER, [(0, 1), (1, 0), (3, 2)])]
  transfers between devices with their start and end apart: 5 -> 5, of which waited for: 2 -> 1; matrix products, arithmetic and copies ran while one was open for 6% -> 3% of each run, Pallas kernels for 0% -> 4%
where the time goes in v2:
time: 238 us; the launch traced here: 237 us
  blocking collectives  128 us (54%)
  waiting for transfers between devices  32.3 us (14%)
  starting transfers between devices  22.6 us (9%)
  matrix products  19.4 us (8%)
  Pallas kernels  18.4 us (8%)
  local copies, waits for them, and re-layouts  12.8 us (5%)
  other arithmetic  2.7 us (1%)
    all_to_all x1, blocking collectives, body(): parts = lax.all_to_all(sums, SAME_CORE, 0, 0, tiled=True)  65.1 us
    all_to_all x1, blocking collectives, gather_rows(): return lax.all_to_all(copies, axes, 0, 0, tiled=True)  63.3 us
    all_to_all x1, waiting for transfers between devices, gather_rows(): return lax.all_to_all(copies, axes, 0, 0, tiled=True)  32.3 us
    dot_general x6, matrix products, dot(): lax.dot_general(a, b, (((ca,), (cb,)), ((), ())), preferred_element_type=...  19.4 us
    all_to_all x1, starting transfers between devices, gather_rows(): return lax.all_to_all(copies, axes, 0, 0, tiled=True)  11 us
    pallas_call x1, Pallas kernels, backward_other(): pl.pallas_call(other_kernel, grid_spec=pltpu.PrefetchScalarGridSpec(num_s...  9.69 us
    pallas_call x1, Pallas kernels, backward_own(): pl.pallas_call(own_kernel, grid_spec=pltpu.PrefetchScalarGridSpec(num_sca...  8.76 us
    unnamed x13, local copies, waits for them, and re-layouts  8.18 us
  transfers between devices with their start and end apart: 5, of which 1 were waited for; matrix products, arithmetic and copies ran while one was open for 3% of the time, Pallas kernels for 4%

profile of v2, /device:TPU:0, one launch (start us, length us, event | category | flops | bytes accessed | tf_op | source)
XLA Modules:
  0.0 237.5 jit_solution(11871208108970788908)
XLA Ops:
  0.6 0.0 copy-start
  0.6 2.6 %broadcast_in_dim.12 = bf16[32,144,256]{2,1,0:T(8,128)(2,1)} broadcast(bf16[144,256]{1,0:T(8,128)(2,1)} %bitcast.76), dimensions={1,2} | broadcast | bytes 2433024 | tf_op jit(solution)/shard_map/broadcast_in_dim | solution.py:24
  3.2 0.0 copy-start.5
  3.2 11.0 %all-to-all-start = ((bf16[32,144,256]{2,1,0:T(8,128)(2,1)}), bf16[32,144,256]{2,1,0:T(8,128)(2,1)}, u32[]{:S(2)}, u32[]{:S(2)}) async-start(bf16[32,144,256]{2,1,0:T(8,128)(2,1)} %broadcast_in_dim.12), calls=%async_computation | async-start | bytes 4718592 | tf_op jit(solution)/shard_map/all_to_all | solution.py:25
  14.2 32.3 %all-to-all-done = bf16[32,144,256]{2,1,0:T(8,128)(2,1)} async-done(((bf16[32,144,256]{2,1,0:T(8,128)(2,1)}), bf16[32,144,256]{2,1,0:T(8,128)(2,1)}, u32[]{:S(2)}, u32[]{:S(2)}) %all-to-all-start) | async-done | bytes 2359328 | tf_op jit(solution)/shard_map/all_to_all | solution.py:25
  46.5 0.0 copy-done
  46.5 0.0 copy-done.5
  46.5 2.5 %fusion.29 = (bf16[256,256]{1,0:T(8,128)(2,1)S(1)}, f32[256,256]{1,0:T(8,128)S(1)}) fusion(f32[256]{0:T(256)S(1)} %bitcast.80, bf16[4608,256]{1,0:T(8,128)(2,1)} %bitcast.9, bf16[1,4608,256]{2,1,0:T(8,128)(2,1)S(1)} %copy-done), kind=kOutput, calls=%fused_computation.31 | convolution fusion | flops 604635136 | bytes 5112832 | tf_op jit(solution)/shard_map/dot_general | solution.py:20
  49.1 2.5 %convolution_convert_fusion.1 = bf16[4608,256]{1,0:T(8,128)(2,1)S(1)} fusion(bf16[256,256]{1,0:T(8,128)(2,1)S(1)} %get-tuple-element.26.latent_ref, bf16[1,4,256,4608]{3,2,1,0:T(8,128)(2,1)} %param.10, s32[]{:T(128)S(6)} %select_n.26), kind=kOutput, calls=%fused_computation.2 | convolution fusion | flops 605159424 | bytes 4849668 | tf_op jit(solution)/shard_map/dot_general | solution.py:20
  51.6 1.9 collective-permute-start.1
  53.5 3.9 %convolution_convert_fusion.2 = bf16[4608,256]{1,0:T(8,128)(2,1)} fusion(bf16[256,256]{1,0:T(8,128)(2,1)S(1)} %get-tuple-element.26.latent_ref, bf16[1,4,256,4608]{3,2,1,0:T(8,128)(2,1)} %param.10, s32[]{:T(128)S(6)} %select_n.23), kind=kOutput, calls=%fused_computation.3 | convolution fusion | flops 605159424 | bytes 4849668 | tf_op jit(solution)/shard_map/dot_general | solution.py:20
  57.4 3.8 %collective-permute-start = (bf16[4608,256]{1,0:T(8,128)(2,1)}, bf16[4608,256]{1,0:T(8,128)(2,1)}, u32[]{:S(2)}, u32[]{:S(2)}) collective-permute-start(bf16[4608,256]{1,0:T(8,128)(2,1)} %convolution_convert_fusion.2), channel_id=1, source_target_pairs={{0,32},{1,33},{2,34},{3,35},{4,36},{5,37},{6,38},{7,39},{8,40},{9,... | collective-permute-start | bytes 7077896 | tf_op jit(solution)/shard_map/ppermute | solution.py:167
  61.2 0.0 collective-permute-done.1
  61.2 3.2 %fusion.2 = bf16[1,4608,256]{2,1,0:T(8,128)(2,1)S(1)} fusion(bf16[4608,256]{1,0:T(8,128)(2,1)} %collective-permute-done.1, bf16[256,256]{1,0:T(8,128)(2,1)S(1)} %get-tuple-element.26.latent_ref, bf16[1,4,256,4608]{3,2,1,0:T(8,128)(2,1)} %param.10, s32[]{:T(128)S(6)} %select_n.25), kind=kOutput, calls=%fused_computation.9 | convolution fusion | flops 607518720 | bytes 7208964 | tf_op jit(solution)/shard_map/dot_general | solution.py:20
  64.5 0.0 collective-permute-done
  64.5 3.2 %fusion.1 = bf16[1,4608,256]{2,1,0:T(8,128)(2,1)S(1)} fusion(bf16[4608,256]{1,0:T(8,128)(2,1)} %collective-permute-done, bf16[256,256]{1,0:T(8,128)(2,1)S(1)} %get-tuple-element.26.latent_ref, bf16[1,4,256,4608]{3,2,1,0:T(8,128)(2,1)} %param.10, s32[]{:T(128)S(6)} %select_n.22, pred[]{:T(512)S(6)} %eq.4), kind=kOutput, calls=%fused_computation.8 | convolution fusion | flops 608698368 | bytes 7208965 | tf_op jit(solution)/shard_map/dot_general | solution.py:20
  67.7 0.4 pad_maximum_fusion
  68.1 65.1 %all_to_all.15 = bf16[64,144,256]{2,1,0:T(8,128)(2,1)S(1)} all-to-all(bf16[64,144,256]{2,1,0:T(8,128)(2,1)S(1)} %bitcast.74), channel_id=1, replica_groups=mesh['zlo'=2,'core'=2,'zhi'=2,'y'=4,'x'=4] {'zlo','zhi','y','x'}, dimensions={0} | all-to-all | bytes 9437184 | tf_op jit(solution)/shard_map/all_to_all | solution.py:172
  133.3 0.0 copy-start.3
  133.3 0.0 copy-start.4
  133.3 0.7 convert_reduce_fusion
  133.9 0.2 copy-done.3
  134.2 0.0 copy-done.4
  134.2 0.2 fusion.31
  134.3 0.3 broadcast_in_dim.25
  134.7 63.3 %all_to_all.16 = bf16[64,144,256]{2,1,0:T(8,128)(2,1)S(1)} all-to-all(bf16[64,144,256]{2,1,0:T(8,128)(2,1)S(1)} %broadcast_in_dim.25), channel_id=1, replica_groups=mesh['zlo'=2,'core'=2,'zhi'=2,'y'=4,'x'=4] {'zlo','zhi','y','x'}, dimensions={0} | all-to-all | bytes 9437184 | tf_op jit(solution)/shard_map/all_to_all | solution.py:25
  198.0 1.7 fusion.36
  199.7 1.3 collective-permute-start.2
  201.0 4.6 %collective-permute-start.3 = (bf16[4608,256]{1,0:T(8,128)(2,1)}, bf16[4608,256]{1,0:T(8,128)(2,1)}, u32[]{:S(2)}, u32[]{:S(2)}) collective-permute-start(bf16[4608,256]{1,0:T(8,128)(2,1)} %bitcast.21.late_ref), channel_id=1, source_target_pairs={{0,32},{32,0},{96,64},{1,33},{33,1},{97,65},{2,34},{34,2},{98,66},... | collective-permute-start | bytes 7077896 | tf_op jit(solution)/shard_map/ppermute | solution.py:180
  205.6 0.1 pad_add_fusion.plan
  205.7 0.1 pad_add_fusion.1.plan
  205.8 0.6 broadcast_multiply_fusion
  206.3 0.0 copy-start.2
  206.3 3.7 %copy-done.2 = bf16[1,4,256,4608]{3,2,1,0:T(8,128)(2,1)S(1)} copy-done((bf16[1,4,256,4608]{3,2,1,0:T(8,128)(2,1)S(1)}, bf16[1,4,256,4608]{3,2,1,0:T(8,128)(2,1)}, u32[]{:S(2)}) %copy-start.2) | copy-done | bytes 9437208
  210.0 8.8 %backward_own.1 = (bf16[4,256,4608]{2,1,0:T(8,128)(2,1)}, f32[256,256]{1,0:T(8,128)S(1)}) custom-call(s32[4]{0:T(128)S(1)} %pad_add_fusion.1.plan, bf16[4,256,4608]{2,1,0:T(8,128)(2,1)S(1)} %bitcast.70, bf16[4608,256]{1,0:T(8,128)(2,1)S(1)} %bitcast.73, bf16[4608,256]{1,0:T(8,128)(2,1)} %bitcast.21.late_ref, bf16[256,256]{1,0:T(8,128)(2,1)S(1)} %get-tuple-element.26.latent_ref), custom_call_target="tpu_custom_call" | custom-call | flops 2415919104 | bytes 14155776 | tf_op jit(solution)/shard_map/backward_own/pallas_call | solution.py:107
  218.8 0.0 collective-permute-done.2.early_ref
  218.8 0.0 collective-permute-done.3.late_ref
  218.8 9.7 %backward_other.1 = (bf16[4,256,4608]{2,1,0:T(8,128)(2,1)}, bf16[256,256]{1,0:T(8,128)(2,1)S(1)}, f32[256,1]{1,0:T(8,128)S(1)}) custom-call(s32[4]{0:T(128)S(1)} %pad_add_fusion.plan, bf16[4,256,4608]{2,1,0:T(8,128)(2,1)S(1)} %bitcast.71, bf16[4608,256]{1,0:T(8,128)(2,1)} %collective-permute-done.2.early_ref, ...), custom_call_target="tpu_custom_call", output_to_operand_aliasing={{0}: (7, {})} | custom-call | flops 2415919104 | bytes 14155776 | tf_op jit(solution)/shard_map/backward_other/pallas_call | solution.py:126
  228.5 0.0 copy-start.1
  228.5 4.0 %fusion = bf16[1,4608,256]{1,2,0:T(8,128)(2,1)} fusion(bf16[256,256]{1,0:T(8,128)(2,1)S(1)} %get-tuple-element.11, bf16[4608,256]{1,0:T(8,128)(2,1)} %bitcast.9), kind=kOutput, calls=%fused_computation.4 | convolution fusion | flops 605159424 | bytes 4849664 | tf_op jit(solution)/shard_map/dot_general | solution.py:20
  232.5 4.3 %copy.12 = bf16[1,4608,256]{2,1,0:T(8,128)(2,1)} copy(bf16[1,4608,256]{1,2,0:T(8,128)(2,1)} %fusion) | data formatting | bytes 4718592
  236.8 0.7 reduce
  237.5 0.0 copy-done.1
Async XLA Ops:
  0.6 45.9 %copy-start = (bf16[1,4608,256]{2,1,0:T(8,128)(2,1)S(1)}, bf16[1,4608,256]{2,1,0:T(8,128)(2,1)}, u32[]{:S(2)}) copy-start(bf16[1,4608,256]{2,1,0:T(8,128)(2,1)} %param.8) | copy-start | bytes 7077892
  3.2 43.3 %copy-start.5 = (f32[1,256]{1,0:T(1,128)S(1)}, f32[1,256]{1,0:T(1,128)}, u32[]{:S(2)}) copy-start(f32[1,256]{1,0:T(1,128)} %param.9) | copy-start | bytes 3076
  3.2 43.3 %all-to-all-start = ((bf16[32,144,256]{2,1,0:T(8,128)(2,1)}), bf16[32,144,256]{2,1,0:T(8,128)(2,1)}, u32[]{:S(2)}, u32[]{:S(2)}) async-start(bf16[32,144,256]{2,1,0:T(8,128)(2,1)} %broadcast_in_dim.12), calls=%async_computation | async-start | bytes 4718592 | tf_op jit(solution)/shard_map/all_to_all | solution.py:25
  51.6 9.7 %collective-permute-start.1 = (bf16[4608,256]{1,0:T(8,128)(2,1)S(1)}, bf16[4608,256]{1,0:T(8,128)(2,1)}, u32[]{:S(2)}, u32[]{:S(2)}) collective-permute-start(bf16[4608,256]{1,0:T(8,128)(2,1)S(1)} %convolution_convert_fusion.1), channel_id=1, source_target_pairs={{0,32},{32,0},{64,96},{1,33},{33,1},{65,97},{2,34},{34,2},{66,98},... | collective-permute-start | bytes 7077896 | tf_op jit(solution)/shard_map/ppermute | solution.py:165
  57.4 7.1 %collective-permute-start = (bf16[4608,256]{1,0:T(8,128)(2,1)}, bf16[4608,256]{1,0:T(8,128)(2,1)}, u32[]{:S(2)}, u32[]{:S(2)}) collective-permute-start(bf16[4608,256]{1,0:T(8,128)(2,1)} %convolution_convert_fusion.2), channel_id=1, source_target_pairs={{0,32},{1,33},{2,34},{3,35},{4,36},{5,37},{6,38},{7,39},{8,40},{9,... | collective-permute-start | bytes 7077896 | tf_op jit(solution)/shard_map/ppermute | solution.py:167
  133.3 0.9 copy-start.3
  133.3 0.9 copy-start.4
  199.7 19.1 %collective-permute-start.2 = (bf16[4608,256]{1,0:T(8,128)(2,1)S(1)}, bf16[4608,256]{1,0:T(8,128)(2,1)}, u32[]{:S(2)}, u32[]{:S(2)}) collective-permute-start(bf16[4608,256]{1,0:T(8,128)(2,1)S(1)} %bitcast.72), channel_id=1, source_target_pairs={{32,0},{33,1},{34,2},{35,3},{36,4},{37,5},{38,6},{39,7},{40,8},{41... | collective-permute-start | bytes 7077896 | tf_op jit(solution)/shard_map/ppermute | solution.py:181
  201.0 17.8 %collective-permute-start.3 = (bf16[4608,256]{1,0:T(8,128)(2,1)}, bf16[4608,256]{1,0:T(8,128)(2,1)}, u32[]{:S(2)}, u32[]{:S(2)}) collective-permute-start(bf16[4608,256]{1,0:T(8,128)(2,1)} %bitcast.21.late_ref), channel_id=1, source_target_pairs={{0,32},{32,0},{96,64},{1,33},{33,1},{97,65},{2,34},{34,2},{98,66},... | collective-permute-start | bytes 7077896 | tf_op jit(solution)/shard_map/ppermute | solution.py:180
  206.3 3.7 %copy-start.2 = (bf16[1,4,256,4608]{3,2,1,0:T(8,128)(2,1)S(1)}, bf16[1,4,256,4608]{3,2,1,0:T(8,128)(2,1)}, u32[]{:S(2)}) copy-start(bf16[1,4,256,4608]{3,2,1,0:T(8,128)(2,1)} %param.10) | copy-start | bytes 28311556
  228.5 9.0 %copy-start.1 = (bf16[1,4608,256]{2,1,0:T(8,128)(2,1)S(1)}, bf16[1,4608,256]{2,1,0:T(8,128)(2,1)}, u32[]{:S(2)}) copy-start(bf16[1,4608,256]{2,1,0:T(8,128)(2,1)} %param.8) | copy-start | bytes 7077892

commit v3 on v1

v3 whole, which is shorter than its diff:
```python
import math

import jax
import jax.numpy as jnp
from jax import lax
from jax.experimental import pallas as pl
from jax.experimental.pallas import tpu as pltpu
from jax.sharding import Mesh, PartitionSpec as P

LAYER = ("zlo", "core")
LAT = ("zhi", "y", "x")
SAME_CORE = ("zlo", "zhi", "y", "x")
TILE = 1152
AHEAD = 3
ANYWHERE = pl.BlockSpec(memory_space=pl.ANY)
LOCAL = pl.BlockSpec(memory_space=pltpu.VMEM)
PARAMS = pltpu.CompilerParams(vmem_limit_bytes=60 * 1024 * 1024)


def gelu_tanh(values):
    return jax.nn.gelu(values, approximate=True)


def gelu_slope(x):
    scale, cubic = math.sqrt(2.0 / math.pi), 0.044715
    bent = jnp.tanh(scale * (x + cubic * x * x * x))
    return 0.5 * (1.0 + bent) + 0.5 * x * (1.0 - bent * bent) * scale * (1.0 + 3.0 * cubic * x * x)


def dot(a, b, ca, cb):
    return lax.dot_general(a, b, (((ca,), (cb,)), ((), ())), preferred_element_type=jnp.float32)


def gather_rows(block, axes, count):
    copies = jnp.broadcast_to(block[None], (count,) + block.shape)
    return lax.all_to_all(copies, axes, 0, 0, tiled=True)


def buffers(count, *shape):
    return [pltpu.VMEM((count,) + shape, jnp.bfloat16), pltpu.SemaphoreType.DMA((count,))]


def place():
    return lax.axis_index("zlo"), lax.axis_index("core")


def decode(dec, lent, latent, lent_latent):
    _, rows, width = dec.shape
    tokens = latent.shape[1]
    tiles = width // TILE
    steps = 2 * tiles

    def kernel(dec_ref, lent_ref, latent_ref, lent_latent_ref, sums_ref,
               own_buf, own_sem, lent_buf, lent_sem, out_buf, out_sem):
        zlo, core = place()

        def live(step):
            return (zlo == 0) | (step >= tiles)

        def lent_live(step):
            return (core == 1) | (zlo == 0) if step >= tiles else (core == 1) & (zlo == 0)

        def source(ref, step):
            return ref.at[core + 2 * (step // tiles), :, pl.ds(step % tiles * TILE, TILE)]

        def own_copy(step):
            return pltpu.make_async_copy(source(dec_ref, step), own_buf.at[step], own_sem.at[step])

        def lent_copy(step):
            return pltpu.make_async_copy(source(lent_ref, step), lent_buf.at[step], lent_sem.at[step])

        def out_copy(step):
            block = sums_ref.at[step // tiles, pl.ds(step % tiles * TILE, TILE)]
            return pltpu.make_async_copy(out_buf.at[step], block, out_sem.at[step])

        def begin(step):
            @pl.when(live(step))
            def _():
                own_copy(step).start()

            @pl.when(lent_live(step))
            def _():
                lent_copy(step).start()

        for step in range(AHEAD):
            begin(step)
        for step in range(steps):
            if step + AHEAD < steps:
                begin(step + AHEAD)

            @pl.when(live(step))
            def _(step=step):
                own_copy(step).wait()
                own = dot(own_buf[step], latent_ref[...], 0, 0)

                @pl.when(lent_live(step))
                def _():
                    lent_copy(step).wait()
                    both = own + dot(lent_buf[step], lent_latent_ref[...], 0, 0)
                    out_buf[step] = both.astype(jnp.bfloat16)

                @pl.when(jnp.logical_not(lent_live(step)))
                def _():
                    out_buf[step] = own.astype(jnp.bfloat16)

            @pl.when(jnp.logical_not(live(step)))
            def _(step=step):
                out_buf[step] = jnp.zeros((TILE, tokens), jnp.bfloat16)

            out_copy(step).start()
        for step in range(steps):
            out_copy(step).wait()

    return pl.pallas_call(
        kernel,
        in_specs=[ANYWHERE, ANYWHERE, LOCAL, LOCAL],
        out_specs=ANYWHERE,
        scratch_shapes=buffers(steps, rows, TILE) * 2 + buffers(steps, TILE, tokens),
        out_shape=jax.ShapeDtypeStruct((2, width, tokens), jnp.bfloat16),
        compiler_params=PARAMS,
        cost_estimate=pl.CostEstimate(
            flops=8 * rows * width * tokens, bytes_accessed=12 * rows * width, transcendentals=0),
        name="decode",
    )(dec, lent, latent, lent_latent)


def backward(dec, latent, grads, given=None, finish=None):
    _, rows, width = dec.shape
    tokens = latent.shape[1]
    tiles = width // TILE
    steps = 2 * tiles
    given = given or []
    n_given = len(given)

    def kernel(dec_ref, latent_ref, grads_ref, *refs):
        zlo, core = place()
        first_target = 1 - core if given else core
        given_refs, refs = refs[:n_given], refs[n_given:]
        if finish:
            preact_ref, resid_ref, grad_dec_ref, grad_enc_ref, bias_ref, *refs = refs
            total_ref, resid_buf, resid_sem, enc_buf, enc_sem, *refs = refs
        else:
            grad_dec_ref, total_ref, *refs = refs
        dec_buf, dec_sem, grad_buf, grad_sem, out_buf, out_sem = refs

        def target(step):
            return first_target + 2 * (step // tiles)

        def live(step):
            return target(step) >= 2 * zlo + core

        def columns(step):
            return pl.ds(step % tiles * TILE, TILE)

        def dec_copy(step):
            source = dec_ref.at[target(step), :, columns(step)]
            return pltpu.make_async_copy(source, dec_buf.at[step], dec_sem.at[step])

        def grad_copy(step):
            source = grads_ref.at[step // tiles, columns(step)]
            return pltpu.make_async_copy(source, grad_buf.at[step], grad_sem.at[step])

        def out_copy(step):
            block = grad_dec_ref.at[target(step), :, columns(step)]
            return pltpu.make_async_copy(out_buf.at[step], block, out_sem.at[step])

        def resid_copy(part):
            return pltpu.make_async_copy(resid_ref.at[columns(part)], resid_buf.at[part], resid_sem.at[part])

        def enc_copy(part):
            return pltpu.make_async_copy(enc_buf.at[part], grad_enc_ref.at[columns(part)], enc_sem.at[part])

        def begin(step):
            @pl.when(live(step))
            def _():
                grad_copy(step).start()
                dec_copy(step).start()

        for step in range(AHEAD):
            begin(step)
        total_ref[...] = given_refs[0][...] if given else jnp.zeros_like(total_ref)
        for step in range(steps):
            if step + AHEAD < steps:
                begin(step + AHEAD)
            elif finish and step + AHEAD < steps + tiles:
                resid_copy(step + AHEAD - steps).start()

            @pl.when(live(step))
            def _(step=step):
                grad_copy(step).wait()
                dec_copy(step).wait()
                grad = grad_buf[step]
                total_ref[...] += dot(dec_buf[step], grad, 1, 0)
                out_buf[step] = dot(latent_ref[...], grad, 1, 1).astype(jnp.bfloat16)

            @pl.when(jnp.logical_not(live(step)))
            def _(step=step):
                out_buf[step] = jnp.zeros((rows, TILE), jnp.bfloat16)

            out_copy(step).start()
        if finish:
            for part in range(AHEAD, tiles):
                resid_copy(part).start()
            pre_grad = total_ref[...] * gelu_slope(preact_ref[...])
            bias_ref[...] = jnp.sum(pre_grad.T, axis=0, keepdims=True)
            pre_grad = pre_grad.astype(jnp.bfloat16)
            for part in range(tiles):
                resid_copy(part).wait()
                enc_buf[part] = dot(resid_buf[part], pre_grad, 1, 1).astype(jnp.bfloat16)
                enc_copy(part).start()
        for step in range(steps):
            out_copy(step).wait()
        if finish:
            for part in range(tiles):
                enc_copy(part).wait()

    operands = [dec, latent, grads, *given]
    in_specs = [ANYWHERE, LOCAL, ANYWHERE] + [LOCAL, ANYWHERE][:n_given]
    out_shape = [jax.ShapeDtypeStruct(dec.shape, jnp.bfloat16)]
    out_specs = [ANYWHERE]
    scratch = []
    if finish:
        operands += finish
        in_specs += [LOCAL, ANYWHERE]
        out_shape += [jax.ShapeDtypeStruct((width, rows), jnp.bfloat16), jax.ShapeDtypeStruct((1, rows), jnp.float32)]
        out_specs += [ANYWHERE, LOCAL]
        scratch = [pltpu.VMEM((rows, tokens), jnp.float32)] + buffers(tiles, TILE, tokens) + buffers(tiles, TILE, rows)
    else:
        out_shape += [jax.ShapeDtypeStruct((rows, tokens), jnp.float32)]
        out_specs += [LOCAL]
    scratch += buffers(steps, rows, TILE) + buffers(steps, TILE, tokens) + buffers(steps, rows, TILE)
    return pl.pallas_call(
        kernel,
        in_specs=in_specs,
        out_specs=out_specs,
        scratch_shapes=scratch,
        out_shape=out_shape,
        input_output_aliases={4: 0} if given else {},
        compiler_params=PARAMS,
        cost_estimate=pl.CostEstimate(
            flops=8 * rows * width * tokens, bytes_accessed=12 * rows * width, transcendentals=0),
        name="other_targets" if given else "own_targets",
    )(*operands)


def body(resid, target, enc_weight, enc_bias, dec_weight, dec_bias):
    tokens = resid.shape[1]
    own_rows = resid.shape[2]
    lats = lax.axis_size("zhi") * lax.axis_size("y") * lax.axis_size("x")
    width = own_rows * lats
    factor = 2.0 / tokens
    dec = dec_weight[0]

    lent = lax.ppermute(dec, LAYER, [(0, 1), (1, 0), (2, 3)])

    resid_t = gather_rows(resid[0].T, LAT, lats).reshape(width, tokens)
    resid_t, lent = lax.optimization_barrier((resid_t, lent))
    preact = dot(enc_weight[0], resid_t, 0, 0) + enc_bias[0][:, None]
    latent = gelu_tanh(preact).astype(jnp.bfloat16)
    lent_latent = lax.ppermute(latent, LAYER, [(0, 1), (1, 0), (2, 3), (3, 2)])

    sums = decode(dec, lent, latent, lent_latent)
    parts = lax.all_to_all(sums.reshape(2 * lats, own_rows, tokens), SAME_CORE, 0, 0, tiled=True)
    recon = jnp.sum(parts.astype(jnp.float32), axis=0)

    error = recon + dec_bias[0][:, None] - target[0].T.astype(jnp.float32)
    grad_dec_bias = (factor * jnp.sum(error, axis=1))[None]
    out_grad = (factor * error).astype(jnp.bfloat16)

    grads = gather_rows(out_grad, SAME_CORE, 2 * lats).reshape(2, width, tokens)
    other_grads = lax.ppermute(grads, LAYER, [(0, 1), (1, 0), (3, 2)])

    grad_dec, total = backward(dec, latent, grads)
    grad_dec, grad_enc, bias_grad = backward(dec, latent, other_grads, [total, grad_dec], [preact, resid_t])
    return (grad_enc[None], bias_grad, grad_dec[None], grad_dec_bias)


def solution(mesh):
    fine = Mesh(mesh.devices.reshape(2, 2, 2, 4, 4), LAYER + LAT)
    in_specs = (
        P(LAYER, None, LAT),
        P(LAYER, None, LAT),
        P(LAYER, None, LAT),
        P(LAYER, LAT),
        P(LAYER, None, LAT, None),
        P(LAYER, LAT),
    )
    out_specs = (
        P(LAYER, None, LAT),
        P(LAYER, LAT),
        P(LAYER, None, LAT, None),
        P(LAYER, LAT),
    )
    return jax.shard_map(body, mesh=fine, in_specs=in_specs, out_specs=out_specs, check_vma=False)
```

time: 239 us -> 216 us (0.904)
  blocking collectives: 128 us -> 174 us
  matrix products: 39.2 us -> 2.47 us
  waiting for transfers between devices: 35.1 us -> 1.35 us
  Pallas kernels: 0 us -> 26.9 us
  starting transfers between devices: 20.1 us -> 4.15 us
  other arithmetic: 6.06 us -> 1.43 us
  local copies, waits for them, and re-layouts: 7.3 us -> 4.35 us
    all_to_all x1 -> x2, blocking collectives: 63.3 us -> 109 us  [gather_rows(): return lax.all_to_all(copies, axes, 0, 0, tiled=True)]
    dot_general x14 -> x1, matrix products: 39.2 us -> 2.47 us  [dot(): lax.dot_general(a, b, (((ca,), (cb,)), ((), ())), preferred_element_type=...]
    all_to_all x1 -> x0, waiting for transfers between devices: 32.3 us -> none  [gather_rows(): return lax.all_to_all(copies, axes, 0, 0, tiled=True)]
    pallas_call x0 -> x3, Pallas kernels: none -> 26.9 us  [the longest x2 19.1 us: backward(): pl.pallas_call(kernel, in_specs=in_specs, out_specs=out_specs, scratch_sh...]
    all_to_all x1 -> x0, starting transfers between devices: 11 us -> none  [gather_rows(): return lax.all_to_all(copies, axes, 0, 0, tiled=True)]
    ppermute x4 -> x3, starting transfers between devices: 9.15 us -> 4.15 us  [the longest x1 2.09 us: body(): other_grads = lax.ppermute(grads, LAYER, [(0, 1), (1, 0), (3, 2)])]
    broadcast_in_dim x1 -> x0, other arithmetic: 4.2 us -> none  [body(): grad_dec = jnp.stack(grad_dec)[None]]
  transfers between devices with their start and end apart: 5 -> 3, of which waited for: 2 -> 1; matrix products, arithmetic and copies ran while one was open for 6% -> 1% of each run, Pallas kernels for 0% -> 4%
where the time goes in v3:
time: 216 us; the launch traced here: 215 us
  blocking collectives  174 us (81%)
  Pallas kernels  26.9 us (12%)
  local copies, waits for them, and re-layouts  4.35 us (2%)
  starting transfers between devices  4.15 us (2%)
  matrix products  2.47 us (1%)
    all_to_all x2, blocking collectives, gather_rows(): return lax.all_to_all(copies, axes, 0, 0, tiled=True)  109 us
    all_to_all x1, blocking collectives, body(): lax.all_to_all(sums.reshape(2 * lats, own_rows, tokens), SAME_CORE, 0, 0,...  64.8 us
    pallas_call x2, Pallas kernels, backward(): pl.pallas_call(kernel, in_specs=in_specs, out_specs=out_specs, scratch_sh...  19.1 us
    pallas_call x1, Pallas kernels, decode(): pl.pallas_call(kernel, in_specs=[ANYWHERE, ANYWHERE, LOCAL, LOCAL], out_s...  7.86 us
  transfers between devices with their start and end apart: 3, of which 1 were waited for; matrix products, arithmetic and copies ran while one was open for 1% of the time, Pallas kernels for 4%

profile of v3, /device:TPU:0, one launch (start us, length us, event | category | flops | bytes accessed | tf_op | source)
XLA Modules:
  0.0 215.4 jit_solution(13723387593616440087)
XLA Ops:
  0.6 0.0 copy-start
  0.6 0.0 copy-start.7
  0.7 2.1 collective-permute-start
  2.7 1.0 broadcast_in_dim.8
  3.8 44.0 %all_to_all.15 = bf16[32,144,256]{2,1,0:T(8,128)(2,1)S(1)} all-to-all(bf16[32,144,256]{2,1,0:T(8,128)(2,1)S(1)} %broadcast_in_dim.8), channel_id=1, replica_groups=mesh['zlo'=2,'core'=2,'zhi'=2,'y'=4,'x'=4] {'zhi','y','x'}, dimensions={0} | all-to-all | bytes 4718592 | tf_op jit(solution)/shard_map/all_to_all | solution.py:36
  47.8 0.0 copy-start.1
  47.8 0.0 collective-permute-done.lent_ref
  47.8 0.0 copy-start.2
  47.8 1.4 copy-done.1
  49.2 0.0 copy-done
  49.2 0.0 copy-done.7
  49.2 2.5 %fusion.15 = (bf16[256,256]{1,0:T(8,128)(2,1)S(1)}, f32[256,256]{1,0:T(8,128)}) fusion(f32[256]{0:T(256)S(1)} %bitcast.48, bf16[4608,256]{1,0:T(8,128)(2,1)S(1)} %bitcast.41, bf16[1,4608,256]{2,1,0:T(8,128)(2,1)S(1)} %copy-done), kind=kOutput, calls=%fused_computation.13 | convolution fusion | flops 604635136 | bytes 5112832 | tf_op jit(solution)/shard_map/dot_general | solution.py:31
  51.7 0.7 copy-done.2
  52.4 0.0 copy-start.3
  52.4 0.0 collective-permute-start.1
  52.4 1.3 collective-permute-done.1.lent_latent_ref
  53.8 0.0 copy-done.3
  53.8 0.0 copy-start.4
  53.8 0.7 copy-done.4
  54.4 7.9 %decode.1 = bf16[2,4608,256]{2,1,0:T(8,128)(2,1)} custom-call(bf16[4,256,4608]{2,1,0:T(8,128)(2,1)} %bitcast.37, bf16[4,256,4608]{2,1,0:T(8,128)(2,1)} %copy-done.2, bf16[256,256]{1,0:T(8,128)(2,1)} %copy-done.3, bf16[256,256]{1,0:T(8,128)(2,1)} %copy-done.4), custom_call_target="tpu_custom_call" | custom-call | flops 2415919104 | bytes 14155776 | tf_op jit(solution)/shard_map/decode/pallas_call | solution.py:114
  62.3 64.8 %all_to_all.16 = bf16[64,144,256]{2,1,0:T(8,128)(2,1)S(1)} all-to-all(bf16[64,144,256]{2,1,0:T(8,128)(2,1)} %bitcast.40), channel_id=1, replica_groups=mesh['zlo'=2,'core'=2,'zhi'=2,'y'=4,'x'=4] {'zlo','zhi','y','x'}, dimensions={0} | all-to-all | bytes 9437184 | tf_op jit(solution)/shard_map/all_to_all | solution.py:263
  127.1 0.0 copy-start.5
  127.1 0.0 copy-start.6
  127.1 0.7 convert_reduce_fusion
  127.8 0.2 copy-done.5
  128.0 0.0 copy-done.6
  128.0 0.2 fusion.17
  128.2 0.3 broadcast_in_dim.9
  128.5 65.0 %all_to_all.17 = bf16[64,144,256]{2,1,0:T(8,128)(2,1)} all-to-all(bf16[64,144,256]{2,1,0:T(8,128)(2,1)S(1)} %broadcast_in_dim.9), channel_id=1, replica_groups=mesh['zlo'=2,'core'=2,'zhi'=2,'y'=4,'x'=4] {'zlo','zhi','y','x'}, dimensions={0} | all-to-all | bytes 9437184 | tf_op jit(solution)/shard_map/all_to_all | solution.py:36
  193.5 2.1 collective-permute-start.2
  195.6 0.6 broadcast_multiply_fusion
  196.2 8.4 %own_targets.1 = (bf16[4,256,4608]{2,1,0:T(8,128)(2,1)}, f32[256,256]{1,0:T(8,128)}) custom-call(bf16[4,256,4608]{2,1,0:T(8,128)(2,1)} %bitcast.38, bf16[256,256]{1,0:T(8,128)(2,1)} %copy-done.3, bf16[2,4608,256]{2,1,0:T(8,128)(2,1)} %bitcast.11.grads_ref), custom_call_target="tpu_custom_call" | custom-call | flops 2415919104 | bytes 14155776 | tf_op jit(solution)/shard_map/own_targets/pallas_call | solution.py:232
  204.5 0.0 collective-permute-done.2.grads_ref
  204.6 10.7 %other_targets.1 = (bf16[4,256,4608]{2,1,0:T(8,128)(2,1)}, bf16[4608,256]{1,0:T(8,128)(2,1)}, f32[1,256]{1,0:T(1,128)}) custom-call(bf16[4,256,4608]{2,1,0:T(8,128)(2,1)} %bitcast.39, bf16[256,256]{1,0:T(8,128)(2,1)} %copy-done.3, bf16[2,4608,256]{2,1,0:T(8,128)(2,1)} %collective-permute-done.2.grads_ref, ...), custom_call_target="tpu_custom_call", output_to_operand_aliasing={{0}: (4, {})} | custom-call | flops 2415919104 | bytes 14155776 | tf_op jit(solution)/shard_map/other_targets/pallas_call | solution.py:232
Async XLA Ops:
  0.6 48.6 %copy-start = (bf16[1,4608,256]{2,1,0:T(8,128)(2,1)S(1)}, bf16[1,4608,256]{2,1,0:T(8,128)(2,1)}, u32[]{:S(2)}) copy-start(bf16[1,4608,256]{2,1,0:T(8,128)(2,1)} %param.8) | copy-start | bytes 7077892
  0.6 48.6 %copy-start.7 = (f32[1,256]{1,0:T(1,128)S(1)}, f32[1,256]{1,0:T(1,128)}, u32[]{:S(2)}) copy-start(f32[1,256]{1,0:T(1,128)} %param.9) | copy-start | bytes 3076
  0.7 47.2 %collective-permute-start = (bf16[4,256,4608]{2,1,0:T(8,128)(2,1)}, bf16[4,256,4608]{2,1,0:T(8,128)(2,1)S(1)}, u32[]{:S(2)}, u32[]{:S(2)}) collective-permute-start(bf16[4,256,4608]{2,1,0:T(8,128)(2,1)} %bitcast.36), channel_id=1, source_target_pairs={{0,32},{32,0},{64,96},{1,33},{33,1},{65,97},{2,34},{34,2},{66,98},... | collective-permute-start | bytes 28311560 | tf_op jit(solution)/shard_map/ppermute | solution.py:254
  47.8 1.4 copy-start.1
  47.8 4.6 %copy-start.2 = (bf16[4,256,4608]{2,1,0:T(8,128)(2,1)}, bf16[4,256,4608]{2,1,0:T(8,128)(2,1)S(1)}, u32[]{:S(2)}) copy-start(bf16[4,256,4608]{2,1,0:T(8,128)(2,1)S(1)} %collective-permute-done.lent_ref) | copy-start | bytes 28311556
  52.4 1.4 copy-start.3
  52.4 1.3 collective-permute-start.1
  53.8 0.7 copy-start.4
  127.1 0.9 copy-start.5
  127.1 0.9 copy-start.6
  193.5 11.0 %collective-permute-start.2 = (bf16[2,4608,256]{2,1,0:T(8,128)(2,1)}, bf16[2,4608,256]{2,1,0:T(8,128)(2,1)}, u32[]{:S(2)}, u32[]{:S(2)}) collective-permute-start(bf16[2,4608,256]{2,1,0:T(8,128)(2,1)} %bitcast.11.grads_ref), channel_id=1, source_target_pairs={{0,32},{32,0},{96,64},{1,33},{33,1},{97,65},{2,34},{34,2},{98,66},... | collective-permute-start | bytes 14155784 | tf_op jit(solution)/shard_map/ppermute | solution.py:271

commit v4 on v3

--- a/solution.py
+++ b/solution.py
@@ -11,10 +11,9 @@
 LAT = ("zhi", "y", "x")
 SAME_CORE = ("zlo", "zhi", "y", "x")
 TILE = 1152
-AHEAD = 3
 ANYWHERE = pl.BlockSpec(memory_space=pl.ANY)
 LOCAL = pl.BlockSpec(memory_space=pltpu.VMEM)
-PARAMS = pltpu.CompilerParams(vmem_limit_bytes=60 * 1024 * 1024)
+PARAMS = pltpu.CompilerParams(vmem_limit_bytes=14 * 1024 * 1024)
 
 
 def gelu_tanh(values):
@@ -50,8 +49,7 @@
     tiles = width // TILE
     steps = 2 * tiles
 
-    def kernel(dec_ref, lent_ref, latent_ref, lent_latent_ref, sums_ref,
-               own_buf, own_sem, lent_buf, lent_sem, out_buf, out_sem):
+    def kernel(dec_ref, lent_ref, latent_ref, lent_latent_ref, sums_ref):
         zlo, core = place()
 
         def live(step):
@@ -60,62 +58,30 @@
         def lent_live(step):
             return (core == 1) | (zlo == 0) if step >= tiles else (core == 1) & (zlo == 0)
 
-        def source(ref, step):
-            return ref.at[core + 2 * (step // tiles), :, pl.ds(step % tiles * TILE, TILE)]
-
-        def own_copy(step):
-            return pltpu.make_async_copy(source(dec_ref, step), own_buf.at[step], own_sem.at[step])
-
-        def lent_copy(step):
-            return pltpu.make_async_copy(source(lent_ref, step), lent_buf.at[step], lent_sem.at[step])
-
-        def out_copy(step):
-            block = sums_ref.at[step // tiles, pl.ds(step % tiles * TILE, TILE)]
-            return pltpu.make_async_copy(out_buf.at[step], block, out_sem.at[step])
-
-        def begin(step):
-            @pl.when(live(step))
-            def _():
-                own_copy(step).start()
-
-            @pl.when(lent_live(step))
-            def _():
-                lent_copy(step).start()
-
-        for step in range(AHEAD):
-            begin(step)
+        def columns(step):
+            return pl.ds(step % tiles * TILE, TILE)
+
+        def product(ref, latent_ref, step):
+            return dot(ref[core + 2 * (step // tiles), :, columns(step)], latent_ref[...], 0, 0)
+
         for step in range(steps):
-            if step + AHEAD < steps:
-                begin(step + AHEAD)
-
-            @pl.when(live(step))
-            def _(step=step):
-                own_copy(step).wait()
-                own = dot(own_buf[step], latent_ref[...], 0, 0)
-
-                @pl.when(lent_live(step))
-                def _():
-                    lent_copy(step).wait()
-                    both = own + dot(lent_buf[step], lent_latent_ref[...], 0, 0)
-                    out_buf[step] = both.astype(jnp.bfloat16)
-
-                @pl.when(jnp.logical_not(lent_live(step)))
-                def _():
-                    out_buf[step] = own.astype(jnp.bfloat16)
+            @pl.when(live(step) & lent_live(step))
+            def _(step=step):
+                both = product(dec_ref, latent_ref, step) + product(lent_ref, lent_latent_ref, step)
+                sums_ref[step // tiles, columns(step)] = both.astype(jnp.bfloat16)
+
+            @pl.when(live(step) & jnp.logical_not(lent_live(step)))
+            def _(step=step):
+                sums_ref[step // tiles, columns(step)] = product(dec_ref, latent_ref, step).astype(jnp.bfloat16)
 
             @pl.when(jnp.logical_not(live(step)))
             def _(step=step):
-                out_buf[step] = jnp.zeros((TILE, tokens), jnp.bfloat16)
-
-            out_copy(step).start()
-        for step in range(steps):
-            out_copy(step).wait()
+                sums_ref[step // tiles, columns(step)] = jnp.zeros((TILE, tokens), jnp.bfloat16)
 
     return pl.pallas_call(
         kernel,
-        in_specs=[ANYWHERE, ANYWHERE, LOCAL, LOCAL],
-        out_specs=ANYWHERE,
-        scratch_shapes=buffers(steps, rows, TILE) * 2 + buffers(steps, TILE, tokens),
+        in_specs=[LOCAL, LOCAL, LOCAL, LOCAL],
+        out_specs=LOCAL,
         out_shape=jax.ShapeDtypeStruct((2, width, tokens), jnp.bfloat16),
         compiler_params=PARAMS,
         cost_estimate=pl.CostEstimate(
@@ -138,10 +104,10 @@
         given_refs, refs = refs[:n_given], refs[n_given:]
         if finish:
             preact_ref, resid_ref, grad_dec_ref, grad_enc_ref, bias_ref, *refs = refs
-            total_ref, resid_buf, resid_sem, enc_buf, enc_sem, *refs = refs
+            total_ref, enc_buf, enc_sem, *refs = refs
         else:
             grad_dec_ref, total_ref, *refs = refs
-        dec_buf, dec_sem, grad_buf, grad_sem, out_buf, out_sem = refs
+        out_buf, out_sem = refs
 
         def target(step):
             return first_target + 2 * (step // tiles)
@@ -151,46 +117,20 @@
 
         def columns(step):
             return pl.ds(step % tiles * TILE, TILE)
-
-        def dec_copy(step):
-            source = dec_ref.at[target(step), :, columns(step)]
-            return pltpu.make_async_copy(source, dec_buf.at[step], dec_sem.at[step])
-
-        def grad_copy(step):
-            source = grads_ref.at[step // tiles, columns(step)]
-            return pltpu.make_async_copy(source, grad_buf.at[step], grad_sem.at[step])
 
         def out_copy(step):
             block = grad_dec_ref.at[target(step), :, columns(step)]
             return pltpu.make_async_copy(out_buf.at[step], block, out_sem.at[step])
 
-        def resid_copy(part):
-            return pltpu.make_async_copy(resid_ref.at[columns(part)], resid_buf.at[part], resid_sem.at[part])
-
         def enc_copy(part):
             return pltpu.make_async_copy(enc_buf.at[part], grad_enc_ref.at[columns(part)], enc_sem.at[part])
 
-        def begin(step):
-            @pl.when(live(step))
-            def _():
-                grad_copy(step).start()
-                dec_copy(step).start()
-
-        for step in range(AHEAD):
-            begin(step)
         total_ref[...] = given_refs[0][...] if given else jnp.zeros_like(total_ref)
         for step in range(steps):
-            if step + AHEAD < steps:
-                begin(step + AHEAD)
-            elif finish and step + AHEAD < steps + tiles:
-                resid_copy(step + AHEAD - steps).start()
-
             @pl.when(live(step))
             def _(step=step):
-                grad_copy(step).wait()
-                dec_copy(step).wait()
-                grad = grad_buf[step]
-                total_ref[...] += dot(dec_buf[step], grad, 1, 0)
+                grad = grads_ref[step // tiles, columns(step), :]
+                total_ref[...] += dot(dec_ref[target(step), :, columns(step)], grad, 1, 0)
                 out_buf[step] = dot(latent_ref[...], grad, 1, 1).astype(jnp.bfloat16)
 
             @pl.when(jnp.logical_not(live(step)))
@@ -199,14 +139,11 @@
 
             out_copy(step).start()
         if finish:
-            for part in range(AHEAD, tiles):
-                resid_copy(part).start()
             pre_grad = total_ref[...] * gelu_slope(preact_ref[...])
             bias_ref[...] = jnp.sum(pre_grad.T, axis=0, keepdims=True)
             pre_grad = pre_grad.astype(jnp.bfloat16)
             for part in range(tiles):
-                resid_copy(part).wait()
-                enc_buf[part] = dot(resid_buf[part], pre_grad, 1, 1).astype(jnp.bfloat16)
+                enc_buf[part] = dot(resid_ref[columns(part), :], pre_grad, 1, 1).astype(jnp.bfloat16)
                 enc_copy(part).start()
         for step in range(steps):
             out_copy(step).wait()
@@ -215,20 +152,20 @@
                 enc_copy(part).wait()
 
     operands = [dec, latent, grads, *given]
-    in_specs = [ANYWHERE, LOCAL, ANYWHERE] + [LOCAL, ANYWHERE][:n_given]
+    in_specs = [LOCAL, LOCAL, LOCAL] + [LOCAL, ANYWHERE][:n_given]
     out_shape = [jax.ShapeDtypeStruct(dec.shape, jnp.bfloat16)]
     out_specs = [ANYWHERE]
     scratch = []
     if finish:
         operands += finish
-        in_specs += [LOCAL, ANYWHERE]
+        in_specs += [LOCAL, LOCAL]
         out_shape += [jax.ShapeDtypeStruct((width, rows), jnp.bfloat16), jax.ShapeDtypeStruct((1, rows), jnp.float32)]
         out_specs += [ANYWHERE, LOCAL]
-        scratch = [pltpu.VMEM((rows, tokens), jnp.float32)] + buffers(tiles, TILE, tokens) + buffers(tiles, TILE, rows)
+        scratch = [pltpu.VMEM((rows, tokens), jnp.float32)] + buffers(tiles, TILE, rows)
     else:
         out_shape += [jax.ShapeDtypeStruct((rows, tokens), jnp.float32)]
         out_specs += [LOCAL]
-    scratch += buffers(steps, rows, TILE) + buffers(steps, TILE, tokens) + buffers(steps, rows, TILE)
+    scratch += buffers(steps, rows, TILE)
     return pl.pallas_call(
         kernel,
         in_specs=in_specs,

time: 216 us -> 200 us (0.926)
  Pallas kernels: 26.9 us -> 15 us
  local copies, waits for them, and re-layouts: 4.35 us -> 1.58 us
    pallas_call x2, Pallas kernels: 19.1 us -> 12 us  [backward(): pl.pallas_call(kernel, in_specs=in_specs, out_specs=out_specs, scratch_sh...]
    pallas_call x1, Pallas kernels: 7.86 us -> 2.96 us  [decode(): pl.pallas_call(kernel, in_specs=[LOCAL, LOCAL, LOCAL, LOCAL], out_specs=L...]
    unnamed x16 -> x10, local copies, waits for them, and re-layouts: 3.01 us -> 0.24 us
  transfers between devices with their start and end apart: 3 -> 3, of which waited for: 1 -> 2; matrix products, arithmetic and copies ran while one was open for 1% -> 1% of each run, Pallas kernels for 4% -> 3%
where the time goes in v4:
time: 200 us
  blocking collectives  172 us (86%)
  Pallas kernels  15 us (8%)
  starting transfers between devices  4.23 us (2%)
  waiting for transfers between devices  3.45 us (2%)
    all_to_all x2, blocking collectives, gather_rows(): return lax.all_to_all(copies, axes, 0, 0, tiled=True)  108 us
    all_to_all x1, blocking collectives, body(): lax.all_to_all(sums.reshape(2 * lats, own_rows, tokens), SAME_CORE, 0, 0,...  64.5 us
    pallas_call x2, Pallas kernels, backward(): pl.pallas_call(kernel, in_specs=in_specs, out_specs=out_specs, scratch_sh...  12 us
  transfers between devices with their start and end apart: 3, of which 2 were waited for; matrix products, arithmetic and copies ran while one was open for 1% of the time, Pallas kernels for 3%

profile of v4, /device:TPU:0, one launch (start us, length us, event | category | flops | bytes accessed | tf_op | source)
XLA Modules:
  0.0 199.7 jit_solution(17263841498957711524)
XLA Ops:
  0.6 0.0 copy-start
  0.6 0.0 copy-start.4
  0.7 2.1 %collective-permute-start = (bf16[4,256,4608]{2,1,0:T(8,128)(2,1)}, bf16[4,256,4608]{2,1,0:T(8,128)(2,1)S(1)}, u32[]{:S(2)}, u32[]{:S(2)}) collective-permute-start(bf16[4,256,4608]{2,1,0:T(8,128)(2,1)} %bitcast.36), channel_id=1, source_target_pairs={{0,32},{32,0},{64,96},{1,33},{33,1},{65,97},{2,34},{34,2},{66,98},... | collective-permute-start | bytes 28311560 | tf_op jit(solution)/shard_map/ppermute | solution.py:191
  2.7 1.0 broadcast_in_dim.8
  3.8 0.0 copy-start.1
  3.8 44.3 %all_to_all.15 = bf16[32,144,256]{2,1,0:T(8,128)(2,1)S(1)} all-to-all(bf16[32,144,256]{2,1,0:T(8,128)(2,1)S(1)} %broadcast_in_dim.8), channel_id=1, replica_groups=mesh['zlo'=2,'core'=2,'zhi'=2,'y'=4,'x'=4] {'zhi','y','x'}, dimensions={0} | all-to-all | bytes 4718592 | tf_op jit(solution)/shard_map/all_to_all | solution.py:35
  48.1 0.0 collective-permute-done.lent_ref
  48.1 0.0 copy-done
  48.1 0.0 copy-done.4
  48.1 1.1 fusion.15
  49.2 0.1 collective-permute-start.1
  49.3 1.3 collective-permute-done.1.lent_latent_ref
  50.6 0.0 copy-done.1
  50.6 3.0 %decode.1 = bf16[2,4608,256]{2,1,0:T(8,128)(2,1)S(1)} custom-call(bf16[4,256,4608]{2,1,0:T(8,128)(2,1)S(1)} %bitcast.37, bf16[4,256,4608]{2,1,0:T(8,128)(2,1)S(1)} %collective-permute-done.lent_ref, bf16[256,256]{1,0:T(8,128)(2,1)S(1)} %get-tuple-element.20.latent_ref, bf16[256,256]{1,0:T(8,128)(2,1)S(1)} %collective-permute-done.1.lent_latent_ref), custom_call_target="tpu_custom_call" | custom-call | flops 2415919104 | bytes 14155776 | tf_op jit(solution)/shard_map/decode/pallas_call | solution.py:81
  53.6 64.5 %all_to_all.16 = bf16[64,144,256]{2,1,0:T(8,128)(2,1)S(1)} all-to-all(bf16[64,144,256]{2,1,0:T(8,128)(2,1)S(1)} %bitcast.42), channel_id=1, replica_groups=mesh['zlo'=2,'core'=2,'zhi'=2,'y'=4,'x'=4] {'zlo','zhi','y','x'}, dimensions={0} | all-to-all | bytes 9437184 | tf_op jit(solution)/shard_map/all_to_all | solution.py:200
  118.0 0.0 copy-start.2
  118.0 0.0 copy-start.3
  118.0 0.7 convert_reduce_fusion
  118.7 0.2 copy-done.2
  118.9 0.0 copy-done.3
  118.9 0.2 fusion.17
  119.1 0.3 broadcast_in_dim.9
  119.4 63.3 %all_to_all.17 = bf16[64,144,256]{2,1,0:T(8,128)(2,1)S(1)} all-to-all(bf16[64,144,256]{2,1,0:T(8,128)(2,1)S(1)} %broadcast_in_dim.9), channel_id=1, replica_groups=mesh['zlo'=2,'core'=2,'zhi'=2,'y'=4,'x'=4] {'zlo','zhi','y','x'}, dimensions={0} | all-to-all | bytes 9437184 | tf_op jit(solution)/shard_map/all_to_all | solution.py:35
  182.8 2.1 %collective-permute-start.2 = (bf16[2,4608,256]{2,1,0:T(8,128)(2,1)S(1)}, bf16[2,4608,256]{2,1,0:T(8,128)(2,1)S(1)}, u32[]{:S(2)}, u32[]{:S(2)}) collective-permute-start(bf16[2,4608,256]{2,1,0:T(8,128)(2,1)S(1)} %bitcast.40), channel_id=1, source_target_pairs={{0,32},{32,0},{96,64},{1,33},{33,1},{97,65},{2,34},{34,2},{98,66},... | collective-permute-start | bytes 14155784 | tf_op jit(solution)/shard_map/ppermute | solution.py:208
  184.9 0.6 broadcast_multiply_fusion
  185.4 5.0 %own_targets.1 = (bf16[4,256,4608]{2,1,0:T(8,128)(2,1)}, f32[256,256]{1,0:T(8,128)S(1)}) custom-call(bf16[4,256,4608]{2,1,0:T(8,128)(2,1)S(1)} %bitcast.38, bf16[256,256]{1,0:T(8,128)(2,1)S(1)} %get-tuple-element.20.latent_ref, bf16[2,4608,256]{2,1,0:T(8,128)(2,1)S(1)} %bitcast.41), custom_call_target="tpu_custom_call" | custom-call | flops 2415919104 | bytes 14155776 | tf_op jit(solution)/shard_map/own_targets/pallas_call | solution.py:169
  190.4 2.1 %collective-permute-done.2.grads_ref = bf16[2,4608,256]{2,1,0:T(8,128)(2,1)S(1)} collective-permute-done((bf16[2,4608,256]{2,1,0:T(8,128)(2,1)S(1)}, bf16[2,4608,256]{2,1,0:T(8,128)(2,1)S(1)}, u32[]{:S(2)}, u32[]{:S(2)}) %collective-permute-start.2) | collective-permute-done | bytes 4718624 | tf_op jit(solution)/shard_map/ppermute | solution.py:208
  192.6 7.0 %other_targets.1 = (bf16[4,256,4608]{2,1,0:T(8,128)(2,1)}, bf16[4608,256]{1,0:T(8,128)(2,1)}, f32[1,256]{1,0:T(1,128)}) custom-call(bf16[4,256,4608]{2,1,0:T(8,128)(2,1)S(1)} %bitcast.39, bf16[256,256]{1,0:T(8,128)(2,1)S(1)} %get-tuple-element.20.latent_ref, ...), custom_call_target="tpu_custom_call", output_to_operand_aliasing={{0}: (4, {})} | custom-call | flops 2415919104 | bytes 14155776 | tf_op jit(solution)/shard_map/other_targets/pallas_call | solution.py:169
Async XLA Ops:
  0.6 47.5 %copy-start = (bf16[1,4608,256]{2,1,0:T(8,128)(2,1)S(1)}, bf16[1,4608,256]{2,1,0:T(8,128)(2,1)}, u32[]{:S(2)}) copy-start(bf16[1,4608,256]{2,1,0:T(8,128)(2,1)} %param.8) | copy-start | bytes 7077892
  0.6 47.4 %copy-start.4 = (f32[1,256]{1,0:T(1,128)S(1)}, f32[1,256]{1,0:T(1,128)}, u32[]{:S(2)}) copy-start(f32[1,256]{1,0:T(1,128)} %param.9) | copy-start | bytes 3076
  0.7 47.4 %collective-permute-start = (bf16[4,256,4608]{2,1,0:T(8,128)(2,1)}, bf16[4,256,4608]{2,1,0:T(8,128)(2,1)S(1)}, u32[]{:S(2)}, u32[]{:S(2)}) collective-permute-start(bf16[4,256,4608]{2,1,0:T(8,128)(2,1)} %bitcast.36), channel_id=1, source_target_pairs={{0,32},{32,0},{64,96},{1,33},{33,1},{65,97},{2,34},{34,2},{66,98},... | collective-permute-start | bytes 28311560 | tf_op jit(solution)/shard_map/ppermute | solution.py:191
  3.8 46.8 %copy-start.1 = (bf16[1,4,256,4608]{3,2,1,0:T(8,128)(2,1)S(1)}, bf16[1,4,256,4608]{3,2,1,0:T(8,128)(2,1)}, u32[]{:S(2)}) copy-start(bf16[1,4,256,4608]{3,2,1,0:T(8,128)(2,1)} %param.10) | copy-start | bytes 28311556
  49.2 1.4 collective-permute-start.1
  118.0 0.9 copy-start.2
  118.0 0.9 copy-start.3
  182.8 9.8 %collective-permute-start.2 = (bf16[2,4608,256]{2,1,0:T(8,128)(2,1)S(1)}, bf16[2,4608,256]{2,1,0:T(8,128)(2,1)S(1)}, u32[]{:S(2)}, u32[]{:S(2)}) collective-permute-start(bf16[2,4608,256]{2,1,0:T(8,128)(2,1)S(1)} %bitcast.40), channel_id=1, source_target_pairs={{0,32},{32,0},{96,64},{1,33},{33,1},{97,65},{2,34},{34,2},{98,66},... | collective-permute-start | bytes 14155784 | tf_op jit(solution)/shard_map/ppermute | solution.py:208

commit v5 on v4

--- a/solution.py
+++ b/solution.py
@@ -10,7 +10,7 @@
 LAYER = ("zlo", "core")
 LAT = ("zhi", "y", "x")
 SAME_CORE = ("zlo", "zhi", "y", "x")
-TILE = 1152
+TILE = 2304
 ANYWHERE = pl.BlockSpec(memory_space=pl.ANY)
 LOCAL = pl.BlockSpec(memory_space=pltpu.VMEM)
 PARAMS = pltpu.CompilerParams(vmem_limit_bytes=14 * 1024 * 1024)

time: 200 us -> 200 us (level)
  transfers between devices with their start and end apart: 3 -> 3, of which waited for: 2 -> 2; matrix products, arithmetic and copies ran while one was open for 1% -> 1% of each run, Pallas kernels for 3% -> 2%
where the time goes in v5:
time: 200 us
  blocking collectives  173 us (86%)
  Pallas kernels  13.3 us (7%)
  waiting for transfers between devices  4.24 us (2%)
  starting transfers between devices  4.05 us (2%)
    all_to_all x2, blocking collectives, gather_rows(): return lax.all_to_all(copies, axes, 0, 0, tiled=True)  109 us
    all_to_all x1, blocking collectives, body(): lax.all_to_all(sums.reshape(2 * lats, own_rows, tokens), SAME_CORE, 0, 0,...  64.7 us
    pallas_call x2, Pallas kernels, backward(): pl.pallas_call(kernel, in_specs=in_specs, out_specs=out_specs, scratch_sh...  10.8 us
  transfers between devices with their start and end apart: 3, of which 2 were waited for; matrix products, arithmetic and copies ran while one was open for 1% of the time, Pallas kernels for 2%

profile of v5, /device:TPU:0, one launch (start us, length us, event | category | flops | bytes accessed | tf_op | source)
XLA Modules:
  0.0 199.8 jit_solution(16170180701182519248)
XLA Ops:
  0.6 0.0 copy-start
  0.6 0.0 copy-start.4
  0.7 2.1 %collective-permute-start = (bf16[4,256,4608]{2,1,0:T(8,128)(2,1)}, bf16[4,256,4608]{2,1,0:T(8,128)(2,1)S(1)}, u32[]{:S(2)}, u32[]{:S(2)}) collective-permute-start(bf16[4,256,4608]{2,1,0:T(8,128)(2,1)} %bitcast.36), channel_id=1, source_target_pairs={{0,32},{32,0},{64,96},{1,33},{33,1},{65,97},{2,34},{34,2},{66,98},... | collective-permute-start | bytes 28311560 | tf_op jit(solution)/shard_map/ppermute | solution.py:191
  2.7 1.0 broadcast_in_dim.8
  3.8 0.0 copy-start.1
  3.8 44.3 %all_to_all.15 = bf16[32,144,256]{2,1,0:T(8,128)(2,1)S(1)} all-to-all(bf16[32,144,256]{2,1,0:T(8,128)(2,1)S(1)} %broadcast_in_dim.8), channel_id=1, replica_groups=mesh['zlo'=2,'core'=2,'zhi'=2,'y'=4,'x'=4] {'zhi','y','x'}, dimensions={0} | all-to-all | bytes 4718592 | tf_op jit(solution)/shard_map/all_to_all | solution.py:35
  48.1 0.0 collective-permute-done.lent_ref
  48.1 0.0 copy-done
  48.1 0.0 copy-done.4
  48.1 1.1 fusion.15
  49.2 0.1 collective-permute-start.1
  49.3 1.3 collective-permute-done.1.lent_latent_ref
  50.6 0.0 copy-done.1
  50.6 2.5 %decode.1 = bf16[2,4608,256]{2,1,0:T(8,128)(2,1)S(1)} custom-call(bf16[4,256,4608]{2,1,0:T(8,128)(2,1)S(1)} %bitcast.37, bf16[4,256,4608]{2,1,0:T(8,128)(2,1)S(1)} %collective-permute-done.lent_ref, bf16[256,256]{1,0:T(8,128)(2,1)S(1)} %get-tuple-element.20.latent_ref, bf16[256,256]{1,0:T(8,128)(2,1)S(1)} %collective-permute-done.1.lent_latent_ref), custom_call_target="tpu_custom_call" | custom-call | flops 2415919104 | bytes 14155776 | tf_op jit(solution)/shard_map/decode/pallas_call | solution.py:81
  53.1 64.7 %all_to_all.16 = bf16[64,144,256]{2,1,0:T(8,128)(2,1)S(1)} all-to-all(bf16[64,144,256]{2,1,0:T(8,128)(2,1)S(1)} %bitcast.42), channel_id=1, replica_groups=mesh['zlo'=2,'core'=2,'zhi'=2,'y'=4,'x'=4] {'zlo','zhi','y','x'}, dimensions={0} | all-to-all | bytes 9437184 | tf_op jit(solution)/shard_map/all_to_all | solution.py:200
  117.8 0.0 copy-start.2
  117.8 0.0 copy-start.3
  117.8 0.7 convert_reduce_fusion
  118.5 0.2 copy-done.2
  118.7 0.0 copy-done.3
  118.7 0.2 fusion.17
  118.9 0.3 broadcast_in_dim.9
  119.2 64.3 %all_to_all.17 = bf16[64,144,256]{2,1,0:T(8,128)(2,1)S(1)} all-to-all(bf16[64,144,256]{2,1,0:T(8,128)(2,1)S(1)} %broadcast_in_dim.9), channel_id=1, replica_groups=mesh['zlo'=2,'core'=2,'zhi'=2,'y'=4,'x'=4] {'zlo','zhi','y','x'}, dimensions={0} | all-to-all | bytes 9437184 | tf_op jit(solution)/shard_map/all_to_all | solution.py:35
  183.4 1.9 collective-permute-start.2
  185.4 0.6 broadcast_multiply_fusion
  185.9 4.4 %own_targets.1 = (bf16[4,256,4608]{2,1,0:T(8,128)(2,1)}, f32[256,256]{1,0:T(8,128)S(1)}) custom-call(bf16[4,256,4608]{2,1,0:T(8,128)(2,1)S(1)} %bitcast.38, bf16[256,256]{1,0:T(8,128)(2,1)S(1)} %get-tuple-element.20.latent_ref, bf16[2,4608,256]{2,1,0:T(8,128)(2,1)S(1)} %bitcast.41), custom_call_target="tpu_custom_call" | custom-call | flops 2415919104 | bytes 14155776 | tf_op jit(solution)/shard_map/own_targets/pallas_call | solution.py:169
  190.3 2.9 %collective-permute-done.2.grads_ref = bf16[2,4608,256]{2,1,0:T(8,128)(2,1)S(1)} collective-permute-done((bf16[2,4608,256]{2,1,0:T(8,128)(2,1)S(1)}, bf16[2,4608,256]{2,1,0:T(8,128)(2,1)S(1)}, u32[]{:S(2)}, u32[]{:S(2)}) %collective-permute-start.2) | collective-permute-done | bytes 4718624 | tf_op jit(solution)/shard_map/ppermute | solution.py:208
  193.2 6.4 %other_targets.1 = (bf16[4,256,4608]{2,1,0:T(8,128)(2,1)}, bf16[4608,256]{1,0:T(8,128)(2,1)}, f32[1,256]{1,0:T(1,128)}) custom-call(bf16[4,256,4608]{2,1,0:T(8,128)(2,1)S(1)} %bitcast.39, bf16[256,256]{1,0:T(8,128)(2,1)S(1)} %get-tuple-element.20.latent_ref, ...), custom_call_target="tpu_custom_call", output_to_operand_aliasing={{0}: (4, {})} | custom-call | flops 2415919104 | bytes 14155776 | tf_op jit(solution)/shard_map/other_targets/pallas_call | solution.py:169
Async XLA Ops:
  0.6 47.5 %copy-start = (bf16[1,4608,256]{2,1,0:T(8,128)(2,1)S(1)}, bf16[1,4608,256]{2,1,0:T(8,128)(2,1)}, u32[]{:S(2)}) copy-start(bf16[1,4608,256]{2,1,0:T(8,128)(2,1)} %param.8) | copy-start | bytes 7077892
  0.6 47.4 %copy-start.4 = (f32[1,256]{1,0:T(1,128)S(1)}, f32[1,256]{1,0:T(1,128)}, u32[]{:S(2)}) copy-start(f32[1,256]{1,0:T(1,128)} %param.9) | copy-start | bytes 3076
  0.7 47.4 %collective-permute-start = (bf16[4,256,4608]{2,1,0:T(8,128)(2,1)}, bf16[4,256,4608]{2,1,0:T(8,128)(2,1)S(1)}, u32[]{:S(2)}, u32[]{:S(2)}) collective-permute-start(bf16[4,256,4608]{2,1,0:T(8,128)(2,1)} %bitcast.36), channel_id=1, source_target_pairs={{0,32},{32,0},{64,96},{1,33},{33,1},{65,97},{2,34},{34,2},{66,98},... | collective-permute-start | bytes 28311560 | tf_op jit(solution)/shard_map/ppermute | solution.py:191
  3.8 46.8 %copy-start.1 = (bf16[1,4,256,4608]{3,2,1,0:T(8,128)(2,1)S(1)}, bf16[1,4,256,4608]{3,2,1,0:T(8,128)(2,1)}, u32[]{:S(2)}) copy-start(bf16[1,4,256,4608]{3,2,1,0:T(8,128)(2,1)} %param.10) | copy-start | bytes 28311556
  49.2 1.4 collective-permute-start.1
  117.8 0.9 copy-start.2
  117.8 0.9 copy-start.3
  183.4 9.8 %collective-permute-start.2 = (bf16[2,4608,256]{2,1,0:T(8,128)(2,1)S(1)}, bf16[2,4608,256]{2,1,0:T(8,128)(2,1)S(1)}, u32[]{:S(2)}, u32[]{:S(2)}) collective-permute-start(bf16[2,4608,256]{2,1,0:T(8,128)(2,1)S(1)} %bitcast.40), channel_id=1, source_target_pairs={{0,32},{32,0},{96,64},{1,33},{33,1},{97,65},{2,34},{34,2},{98,66},... | collective-permute-start | bytes 14155784 | tf_op jit(solution)/shard_map/ppermute | solution.py:208
